TPU v7x, 128 devices: a whole 4x4x4 slice. The times are simulated.
128 devices in a mesh: group: 4 (over y_lo, core), region: 32 (over x, z, y_hi).
Axes of the slice: x: 4, y: 4 (y_hi: 2, y_lo: 2; y = y_hi * 2 + y_lo), z: 4, core: 2. Of those that a mesh axis runs over, the one named last changes fastest.
Arguments:
- object_field: float32 [2, 16384, 2048], P(None, 'region', 'group'), may hold values from -6 to 6
- probe: float32 [2, 4, 256, 256], replicated, may hold values from -2 to 2
- amplitudes: float32 [128, 1024, 256], P('region', 'group'), may hold values from 0.25 to 4
- positions: int32 [128, 8], P('region', 'group'), may hold values from 0 to 256
- dual_top: float32 [2, 2048, 2048], P(None, 'region', 'group'), may hold values from -1.75 to 1.75
- dual_bottom: float32 [2, 2048, 2048], P(None, 'region', 'group'), may hold values from -1.75 to 1.75
- pieces: int32 [64, 4], P('region', 'group'), may hold values from 0 to 3, as said below
- live: int32 [32, 4], P('region', 'group'), may hold values from 1 to 2
Outputs:
- object_new: float32 [2, 16384, 2048], P(None, 'region', 'group')
- probe_new: float32 [2, 4, 256, 256], replicated
- dual_top_new: float32 [2, 2048, 2048], P(None, 'region', 'group')
- dual_bottom_new: float32 [2, 2048, 2048], P(None, 'region', 'group')
Inputs may be any that keep to these rules, and one draw needn't show every extreme that they name: `pieces`: within one tile the 2 listed blocks are distinct.
All inputs are finite; a program needn't handle non-finite values.
Results may differ from a plain program's by a relative error of at most 0.0001.
Values sent between devices are 32-bit elements; how exact they have to be, the bound alone decides.
A program may use at most 128 MiB of HBM per device.

v0:
```python
import numpy as np
import jax
import jax.numpy as jnp
import ml_dtypes
from jax import lax
from jax.experimental import pallas as pl
from jax.experimental.pallas import tpu as pltpu
from jax.sharding import PartitionSpec as P

F32, BF16 = jnp.float32, jnp.bfloat16
MESH = pl.DeviceIdType.MESH
PAT, TILE, MODES, NPAT, HALF = 256, 512, 4, 4, 128
EDGE, BLOCK, NPIECE, KP = 64, 128, 4, 2
SUMS = MODES + 1


def tables():
    n = np.arange(HALF)[:, None]
    out = []
    for p in range(2):
        k = 2 * np.arange(HALF)[None, :] + p
        angle = 2 * np.pi * ((n * k) % PAT) / PAT
        c, s = np.cos(angle) / 16.0, np.sin(angle) / 16.0
        full = np.block([[c, -s], [s, c]])
        out.append(full)
    full = np.stack([np.stack(out), np.stack([o.T for o in out])]).astype(np.float32)
    hi = full.astype(ml_dtypes.bfloat16)
    lo = (full - hi.astype(np.float32)).astype(ml_dtypes.bfloat16)
    perm = np.zeros((PAT, PAT), np.float32)
    for j in range(PAT):
        perm[2 * (j % HALF) + j // HALF, j] = 1.0
    return np.stack([hi, lo], axis=2), np.stack([perm, perm.T]).astype(ml_dtypes.bfloat16)


def dot(a, b):
    return jnp.dot(a, b, preferred_element_type=F32)


def split(a):
    h = a.astype(BF16)
    return h, (a - h.astype(F32)).astype(BF16)


def right(a, t, d, p):
    h, l = split(a)
    return dot(h, t[d, p, 0]) + dot(l, t[d, p, 0]) + dot(h, t[d, p, 1])


def left(t, d, p, a):
    h, l = split(a)
    return dot(t[d, p, 0], h) + dot(t[d, p, 1], h) + dot(t[d, p, 0], l)


def along(shape, axis):
    return lax.broadcasted_iota(jnp.int32, shape, axis)


def lane_turn(block, by):
    return pltpu.roll(block, by & (HALF - 1), 1)


def row_turn(block, by):
    return pltpu.roll(block, by & 7, 1)


def window(obj, plane, row, col):
    base = pl.multiple_of(jnp.minimum((row >> 3) << 3, TILE - PAT - 8), 8)
    side = pl.multiple_of(jnp.minimum((col >> 7) << 7, TILE - PAT - HALF), HALF)
    down, right_by = row - base, col - side
    block = obj[plane, pl.ds(base, PAT + 8), pl.ds(side, PAT + HALF)]
    block = block.reshape((PAT + 8) // 8, 8, PAT + HALF)
    turned = row_turn(block, 8 - down)
    keep = along((PAT // 8, 8, PAT + HALF), 1) + down < 8
    block = jnp.where(keep, turned[:-1], turned[1:]).reshape(PAT, PAT + HALF)
    parts = [lane_turn(block[:, t * HALF:(t + 1) * HALF], HALF - right_by) for t in range(3)]
    keep = along((PAT, HALF), 1) + right_by < HALF
    return jnp.concatenate([jnp.where(keep, parts[t], parts[t + 1]) for t in range(2)], axis=1)


def shifted(block, row, col):
    down, right_by = row & 7, col & (HALF - 1)
    keep = along((PAT, HALF), 1) >= right_by
    left_part = lane_turn(block[:, :HALF], right_by)
    right_part = lane_turn(block[:, HALF:], right_by)
    zero = jnp.zeros_like(left_part)
    block = jnp.concatenate([jnp.where(keep, left_part, zero), jnp.where(keep, right_part, left_part), jnp.where(keep, zero, right_part)], axis=1)
    block = row_turn(block.reshape(PAT // 8, 8, PAT + HALF), down)
    edge = jnp.zeros((1, 8, PAT + HALF), F32)
    above = jnp.concatenate([edge, block], axis=0)
    below = jnp.concatenate([block, edge], axis=0)
    keep = along(below.shape, 1) >= down
    return jnp.where(keep, below, above).reshape(PAT + 8, PAT + HALF)


def prepare(pos, pieces, live, obj, probe, patch, inv, columns, rows, mask, gbuf):
    for j in range(NPAT):
        row, col = pos[j, 0], pos[j, 1]
        for plane in range(2):
            patch[j, plane] = window(obj, plane, row, col)
        columns[j] = (along((PAT, TILE), 1) == along((PAT, TILE), 0) + col).astype(F32).astype(BF16)
        rows[:, j * PAT:(j + 1) * PAT] = (along((TILE, PAT), 0) == along((TILE, PAT), 1) + row).astype(F32).astype(BF16)
    gbuf[...] = jnp.zeros_like(gbuf)
    power = sum(probe[0, m] * probe[0, m] + probe[1, m] * probe[1, m] for m in range(MODES))
    weight = jnp.ones((TILE, TILE), F32)
    for j in range(NPAT):
        row, col = pos[j, 0], pos[j, 1]
        gbuf[pl.ds(PAT, PAT + 8), pl.ds(PAT, PAT + HALF)] = shifted(power, row, col)
        top = pl.multiple_of(PAT - ((row >> 3) << 3), 8)
        side = pl.multiple_of(PAT - ((col >> 7) << 7), HALF)
        weight = weight + gbuf[pl.ds(top, TILE), pl.ds(side, TILE)]
    inv[...] = 1.0 / weight
    count, has_lower = live[0, 0], lax.axis_index("region") < 31
    for b in range(NPIECE):
        hit = ((pieces[0, 0] == b) & (count > 0)) | ((pieces[1, 0] == b) & (count > 1))
        value = jnp.where(hit & has_lower, 1.0, 0.0).astype(F32)
        mask[:, b * BLOCK:(b + 1) * BLOCK] = jnp.full((8, BLOCK), value, F32)


class Place:
    def __init__(self):
        group, region = lax.axis_index("group"), lax.axis_index("region")
        self.group, self.region = group, region
        self.core, y_lo = lax.rem(group, 2), group // 2
        self.x, self.z, y_hi = region // 8, lax.rem(region // 2, 4), lax.rem(region, 2)
        self.y = y_hi * 2 + y_lo
        self.plane = self.x * 4 + self.y

    def at(self, x, y, z, core):
        return (lax.rem(y, 2) * 2 + core, (x * 4 + z) * 2 + y // 2)

    def sibling(self):
        return self.at(self.x, self.y, self.z, 1 - self.core)

    def in_plane(self, k):
        x, y = lax.rem(self.x + k // 4, 4), lax.rem(self.y + lax.rem(k, 4), 4)
        return self.at(x, y, self.z, self.core), x * 4 + y

    def on_line(self, k):
        z = lax.rem(self.z + k, 4)
        return self.at(self.x, self.y, z, self.core), z

    def region_by(self, by):
        return (self.group, lax.rem(self.region + 32 + by, 32))


def send(src, dst, sems, index, device):
    copy = pltpu.make_async_remote_copy(
        src_ref=src, dst_ref=dst, send_sem=sems[0].at[index], recv_sem=sems[1].at[index], device_id=device, device_id_type=MESH
    )
    copy.start()


def await_bytes(ref, sem):
    pltpu.make_async_copy(ref, ref, sem).wait()


def kernel(
    patch, inv, columns, place_rows, mask, obj, probe, amp, dual_top, dual_bottom, tab, perm,
    obj_out, probe_out, top_out, bottom_out,
    far, factor, grad, spread_hi, spread_lo, mid, numer,
    from_core, part, from_plane, line, from_line, own, fresh,
    mask_in, up, low, from_below, from_above, top_new, bottom_new,
    core_send, core_recv, plane_send, plane_recv, line_send, line_recv,
    back_line_send, back_line_recv, back_plane_send, back_plane_recv, back_core_send, back_core_recv,
    edge_send, edge_recv, out_sem,
):
    me = Place()
    barrier = pltpu.get_barrier_semaphore()

    def greet(device):
        pl.semaphore_signal(barrier, inc=1, device_id=device, device_id_type=MESH)

    greet(me.sibling())

    def greet_plane(k, _):
        greet(me.in_plane(k)[0])
        return 0

    lax.fori_loop(1, 16, greet_plane, 0)
    for k in range(1, 4):
        greet(me.on_line(k)[0])
    greet(me.region_by(1))
    greet(me.region_by(-1))

    numer[0, MODES] = jnp.zeros((PAT, PAT), F32)
    grad[...] = jnp.zeros_like(grad)

    def forward(j, _):
        pr, pi = patch[j, 0], patch[j, 1]
        numer[0, MODES] += pr * pr + pi * pi

        def mode(m, _):
            pr, pi = patch[j, 0], patch[j, 1]
            qr, qi = probe[0, m], probe[1, m]
            er = qr * pr - qi * pi
            ei = qr * pi + qi * pr
            lo = jnp.concatenate([er[:, :HALF], ei[:, :HALF]], axis=1)
            hi = jnp.concatenate([er[:, HALF:], ei[:, HALF:]], axis=1)
            y0 = right(lo + hi, tab, 0, 0)
            y1 = right(lo - hi, tab, 0, 1)
            yr = jnp.concatenate([y0[:, :HALF], y1[:, :HALF]], axis=1)
            yi = jnp.concatenate([y0[:, HALF:], y1[:, HALF:]], axis=1)
            top = jnp.concatenate([yr[:HALF], yi[:HALF]], axis=0)
            bot = jnp.concatenate([yr[HALF:], yi[HALF:]], axis=0)
            far[m * NPAT + j, 0] = left(tab, 1, 0, top + bot)
            far[m * NPAT + j, 1] = left(tab, 1, 1, top - bot)
            return 0

        lax.fori_loop(0, MODES, mode, 0)
        h, l = split(amp[j])
        h, l = split(dot(h, perm[0]) + dot(l, perm[0]))
        full = dot(perm[1], h) + dot(perm[1], l)
        for q in range(2):
            power = jnp.zeros((HALF, PAT), F32)
            for m in range(MODES):
                z = far[m * NPAT + j, q]
                power = power + z[:HALF] * z[:HALF] + z[HALF:] * z[HALF:]
            f = full[q * HALF:(q + 1) * HALF] / jnp.maximum(jnp.sqrt(power), 0.5)
            factor[j, q, :HALF] = f
            factor[j, q, HALF:] = f
        return 0

    lax.fori_loop(0, NPAT, forward, 0)

    def inverse(m, first, last):
        def one(j, _):
            g0 = left(tab, 0, 0, far[m * NPAT + j, 0] * factor[j, 0])
            g1 = left(tab, 0, 1, far[m * NPAT + j, 1] * factor[j, 1])
            top, bot = g0 + g1, g0 - g1
            xr = jnp.concatenate([top[:HALF], bot[:HALF]], axis=0)
            xi = jnp.concatenate([top[HALF:], bot[HALF:]], axis=0)
            b0 = right(jnp.concatenate([xr[:, :HALF], xi[:, :HALF]], axis=1), tab, 1, 0)
            b1 = right(jnp.concatenate([xr[:, HALF:], xi[:, HALF:]], axis=1), tab, 1, 1)
            lo, hi = b0 + b1, b0 - b1
            br = jnp.concatenate([lo[:, :HALF], hi[:, :HALF]], axis=1)
            bi = jnp.concatenate([lo[:, HALF:], hi[:, HALF:]], axis=1)
            qr, qi = probe[0, m], probe[1, m]
            grad[j, 0] += qr * br + qi * bi
            grad[j, 1] += qr * bi - qi * br
            pr, pi = patch[j, 0], patch[j, 1]
            numer[0, m] += pr * br + pi * bi
            numer[1, m] += pr * bi - pi * br
            return 0

        if first == 0:
            numer[0, m] = jnp.zeros((PAT, PAT), F32)
            numer[1, m] = jnp.zeros((PAT, PAT), F32)
        lax.fori_loop(first, last, one, 0)

    rows = pl.multiple_of(me.plane * 16, 16)
    core_sems, plane_sems, line_sems = (core_send, core_recv), (plane_send, plane_recv), (line_send, line_recv)
    back_line_sems, back_plane_sems = (back_line_send, back_line_recv), (back_plane_send, back_plane_recv)
    back_core_sems, edge_sems = (back_core_send, back_core_recv), (edge_send, edge_recv)

    def core_start(m):
        plane = 0 if m == MODES else 1 - me.core
        send(numer.at[plane, m], from_core.at[m], core_sems, m, me.sibling())

    def plane_start(m):
        await_bytes(from_core.at[m], core_recv.at[m])
        part[m] = numer[0 if m == MODES else me.core, m] + from_core[m]

        def one(k, _):
            device, number = me.in_plane(k)
            there = pl.multiple_of(number * 16, 16)
            send(part.at[m, pl.ds(there, 16), :], from_plane.at[m, k - 1], plane_sems, m, device)
            return 0

        lax.fori_loop(1, 16, one, 0)

    def line_start(m):
        await_bytes(from_plane.at[m], plane_recv.at[m])
        total = part[m, pl.ds(rows, 16), :]
        for k in range(15):
            total = total + from_plane[m, k]
        for k in range(4):
            line[m, k] = total[(k // 2) * 8:(k // 2) * 8 + 8, (k % 2) * HALF:(k % 2 + 1) * HALF]
        for k in range(1, 4):
            device, there = me.on_line(k)
            send(line.at[m, there], from_line.at[m, k - 1], line_sems, m, device)

    def line_end(m):
        await_bytes(from_line.at[m], line_recv.at[m])
        return line[m, me.z] + from_line[m, 0] + from_line[m, 1] + from_line[m, 2]

    def back_start(m):
        total = line_end(m)
        row = pl.multiple_of(me.plane * 16 + (me.z // 2) * 8, 8)
        column = pl.multiple_of(lax.rem(me.z, 2) * HALF, HALF)
        old = probe[me.core, m, pl.ds(row, 8), pl.ds(column, HALF)]
        own[m, me.z] = (old + total) / (own[MODES, 0] + 1.0)
        for k in range(1, 4):
            send(own.at[m, me.z], own.at[m, me.z], back_line_sems, m, me.on_line(k)[0])

    def back_plane_start(m):
        await_bytes(own.at[m, pl.ds(0, 3)], back_line_recv.at[m])
        top = jnp.concatenate([own[m, 0], own[m, 1]], axis=1)
        bot = jnp.concatenate([own[m, 2], own[m, 3]], axis=1)
        fresh[me.core, m, pl.ds(rows, 16), :] = jnp.concatenate([top, bot], axis=0)
        mine = fresh.at[me.core, m, pl.ds(rows, 16), :]

        def one(k, _):
            send(mine, mine, back_plane_sems, m, me.in_plane(k)[0])
            return 0

        lax.fori_loop(1, 16, one, 0)

    def back_core_start(m):
        await_bytes(fresh.at[me.core, m, pl.ds(0, 240), :], back_plane_recv.at[m])
        send(fresh.at[me.core, m], fresh.at[me.core, m], back_core_sems, m, me.sibling())

    def back_end(m):
        await_bytes(fresh.at[1 - me.core, m], back_core_recv.at[m])
        for plane in range(2):
            pltpu.make_async_copy(fresh.at[plane, m], probe_out.at[plane, m], out_sem.at[plane * MODES + m]).start()

    stages = [core_start, plane_start, line_start, back_start, back_plane_start, back_core_start, back_end]

    def spread(j, _):
        rows = pl.ds(pl.multiple_of(j * PAT, PAT), PAT)
        for plane in range(2):
            h, l = split(grad[j, plane])
            h, l = split(dot(h, columns[j]) + dot(l, columns[j]))
            spread_hi[plane, rows, :] = h
            spread_lo[plane, rows, :] = l
        return 0

    def update(start, count):
        for plane in range(2):
            chosen = place_rows[start:start + count, :]
            total = obj[plane, start:start + count, :] + dot(chosen, spread_hi[plane]) + dot(chosen, spread_lo[plane])
            mid[plane, start:start + count, :] = total * inv[start:start + count, :]

    def mask_start():
        send(mask, mask_in, edge_sems, 0, me.region_by(1))

    def edge_start():
        up[...] = mid[:, :EDGE] + dual_top[...]
        low[...] = mid[:, TILE - EDGE:] + dual_bottom[...]
        send(up, from_below, edge_sems, 1, me.region_by(-1))
        send(low, from_above, edge_sems, 2, me.region_by(1))

    def middle_out():
        middle = pl.ds(EDGE, TILE - 2 * EDGE)
        pltpu.make_async_copy(mid.at[:, middle], obj_out.at[:, middle], out_sem.at[8]).start()

    def edge_end():
        await_bytes(mask_in, edge_recv.at[0])
        await_bytes(from_below, edge_recv.at[1])
        await_bytes(from_above, edge_recv.at[2])
        for plane in range(2):
            here = mid[plane, TILE - EDGE:]
            agreed = 0.5 * (low[plane] + from_below[plane])
            active = jnp.broadcast_to(mask[0:1, :], (EDGE, TILE)) > 0.5
            bottom_new[plane] = jnp.where(active, dual_bottom[plane] + (here - agreed), dual_bottom[plane])
            mid[plane, TILE - EDGE:] = jnp.where(active, agreed, here)
            here = mid[plane, :EDGE]
            agreed = 0.5 * (from_above[plane] + up[plane])
            active = jnp.broadcast_to(mask_in[0:1, :], (EDGE, TILE)) > 0.5
            top_new[plane] = jnp.where(active, dual_top[plane] + (here - agreed), dual_top[plane])
            mid[plane, :EDGE] = jnp.where(active, agreed, here)
        for i, part_rows in enumerate((pl.ds(0, EDGE), pl.ds(TILE - EDGE, EDGE))):
            pltpu.make_async_copy(mid.at[:, part_rows], obj_out.at[:, part_rows], out_sem.at[9 + i]).start()
        pltpu.make_async_copy(top_new, top_out, out_sem.at[11]).start()
        pltpu.make_async_copy(bottom_new, bottom_out, out_sem.at[12]).start()

    pl.semaphore_wait(barrier, 21)
    mask_start()
    core_start(MODES)
    for m in range(MODES):
        inverse(m, 0, 2)
        if m == 0:
            plane_start(MODES)
        if m == 1:
            own[MODES, 0] = line_end(MODES)
            plane_start(0)
        if m == 2:
            back_start(0)
            plane_start(1)
        if m == 3:
            back_core_start(0)
            back_start(1)
            plane_start(2)
        inverse(m, 2, 4)
        if m == 0:
            line_start(MODES)
        if m == 1:
            line_start(0)
        if m == 2:
            back_plane_start(0)
            line_start(1)
        if m == 3:
            back_end(0)
            back_plane_start(1)
            line_start(2)
        core_start(m)
    lax.fori_loop(0, NPAT, spread, 0)
    plane_start(3)
    back_core_start(1)
    back_start(2)
    update(0, EDGE)
    update(TILE - EDGE, EDGE)
    edge_start()
    line_start(3)
    back_end(1)
    back_plane_start(2)
    update(EDGE, 192)
    back_start(3)
    update(EDGE + 192, 192)
    middle_out()
    back_core_start(2)
    back_plane_start(3)
    back_end(2)
    edge_end()
    back_core_start(3)
    back_end(3)

    for m in range(SUMS):
        await_bytes(from_core.at[m], core_send.at[m])
        await_bytes(from_plane.at[m], plane_send.at[m])
        await_bytes(from_line.at[m], line_send.at[m])
    for m in range(MODES):
        await_bytes(own.at[m, pl.ds(0, 3)], back_line_send.at[m])
        await_bytes(fresh.at[0, m, pl.ds(0, 240), :], back_plane_send.at[m])
        await_bytes(fresh.at[0, m], back_core_send.at[m])
        for plane in range(2):
            pltpu.make_async_copy(fresh.at[plane, m], probe_out.at[plane, m], out_sem.at[plane * MODES + m]).wait()
    await_bytes(mask, edge_send.at[0])
    await_bytes(up, edge_send.at[1])
    await_bytes(low, edge_send.at[2])
    middle = pl.ds(EDGE, TILE - 2 * EDGE)
    pltpu.make_async_copy(mid.at[:, middle], obj_out.at[:, middle], out_sem.at[8]).wait()
    for i, part_rows in enumerate((pl.ds(0, EDGE), pl.ds(TILE - EDGE, EDGE))):
        pltpu.make_async_copy(mid.at[:, part_rows], obj_out.at[:, part_rows], out_sem.at[9 + i]).wait()
    pltpu.make_async_copy(top_new, top_out, out_sem.at[11]).wait()
    pltpu.make_async_copy(bottom_new, bottom_out, out_sem.at[12]).wait()


def local(object_field, probe, amplitudes, positions, dual_top, dual_bottom, pieces, live):
    tab, perm = tables()
    vmem = pl.BlockSpec(memory_space=pltpu.VMEM)
    smem = pl.BlockSpec(memory_space=pltpu.SMEM)
    hbm = pl.BlockSpec(memory_space=pl.ANY)
    buf = lambda *shape: pltpu.VMEM(shape, F32)
    half = lambda *shape: pltpu.VMEM(shape, BF16)
    dma = lambda *shape: pltpu.SemaphoreType.DMA(shape)
    edge = (2, EDGE, TILE)
    shape = lambda *dims: jax.ShapeDtypeStruct(dims, F32)
    prepared = pl.pallas_call(
        prepare,
        out_shape=(
            shape(NPAT, 2, PAT, PAT), shape(TILE, TILE), jax.ShapeDtypeStruct((NPAT, PAT, TILE), BF16),
            jax.ShapeDtypeStruct((TILE, NPAT * PAT), BF16), shape(8, TILE),
        ),
        in_specs=[smem] * 3 + [vmem] * 2,
        out_specs=(vmem,) * 5,
        scratch_shapes=[buf(3 * PAT, 3 * PAT)],
        compiler_params=pltpu.CompilerParams(vmem_limit_bytes=40 * 1024 * 1024),
    )(positions, pieces, live, object_field, probe)
    return pl.pallas_call(
        kernel,
        out_shape=(shape(2, TILE, TILE), shape(2, MODES, PAT, PAT), shape(*edge), shape(*edge)),
        in_specs=[vmem] * 12,
        out_specs=(hbm,) * 4,
        scratch_shapes=[
            buf(MODES * NPAT, 2, PAT, PAT), buf(NPAT, 2, PAT, PAT), buf(NPAT, 2, PAT, PAT),
            half(2, NPAT * PAT, TILE), half(2, NPAT * PAT, TILE), buf(2, TILE, TILE), buf(2, SUMS, PAT, PAT),
            buf(SUMS, PAT, PAT), buf(SUMS, PAT, PAT), buf(SUMS, 15, 16, PAT), buf(SUMS, 4, 8, HALF), buf(SUMS, 3, 8, HALF),
            buf(SUMS, 4, 8, HALF), buf(2, MODES, PAT, PAT),
            buf(8, TILE), buf(*edge), buf(*edge), buf(*edge), buf(*edge), buf(*edge), buf(*edge),
        ] + [dma(SUMS)] * 12 + [dma(3), dma(3), dma(13)],
        compiler_params=pltpu.CompilerParams(vmem_limit_bytes=60 * 1024 * 1024, collective_id=0, has_side_effects=True),
    )(*prepared, object_field, probe, amplitudes, dual_top, dual_bottom, jnp.asarray(tab), jnp.asarray(perm))


def solution(mesh):
    tiles = P(None, "region", "group")
    return jax.shard_map(
        local,
        mesh=mesh,
        in_specs=(tiles, P(), P("region", "group", None), P("region", "group"), tiles, tiles, P("region", "group"), P("region", "group")),
        out_specs=(tiles, P(), tiles, tiles),
        check_vma=False,
    )
```

profile of v0, /device:TPU:1, one launch (start us, length us, event | category | flops | bytes accessed | tf_op | source)
XLA Modules:
  0.0 117.2 jit_solution(17399937683187753174)
XLA Ops:
  1.3 0.7 copy.15.pieces
  2.0 0.8 copy.14.pos
  2.8 0.0 copy-start
  2.8 1.6 %copy-done = f32[2,512,512]{2,1,0:T(8,128)S(1)} copy-done((f32[2,512,512]{2,1,0:T(8,128)S(1)}, f32[2,512,512]{2,1,0:T(8,128)}, u32[]{:S(2)}) %copy-start) | copy-done | bytes 2097176
  4.4 0.0 copy-start.1
  4.4 1.6 %copy-done.1 = f32[2,4,256,256]{3,2,1,0:T(8,128)S(1)} copy-done((f32[2,4,256,256]{3,2,1,0:T(8,128)S(1)}, f32[2,4,256,256]{3,2,1,0:T(8,128)}, u32[]{:S(2)}) %copy-start.1) | copy-done | bytes 2097176
  6.0 3.1 %shard_map.129 = (f32[4,2,256,256]{3,2,1,0:T(8,128)S(1)}, f32[512,512]{1,0:T(8,128)S(1)}, bf16[4,256,512]{2,1,0:T(8,128)(2,1)S(1)}, bf16[512,1024]{1,0:T(8,128)(2,1)S(1)}, f32[8,512]{1,0:T(8,128)S(1)}) custom-call(s32[4,2]{1,0:T(4,128)S(1)} %copy.14.pos, s32[2,1]{1,0:T(2,128)S(1)} %copy.15.pieces, s32[1,1]{1,0:T(1,128)S(6)} %copy.20.live, ...), custom_call_target="tpu_custom_call" | custom-call | tf_op jit(solution)/shard_map/pallas_call | solution.py:449
  9.1 0.0 copy-start.2
  9.1 1.3 %copy-done.2 = f32[4,2,256,256]{3,2,1,0:T(8,128)} copy-done((f32[4,2,256,256]{3,2,1,0:T(8,128)}, f32[4,2,256,256]{3,2,1,0:T(8,128)S(1)}, u32[]{:S(2)}) %copy-start.2) | copy-done | bytes 2097176
  10.4 0.0 copy-start.3
  10.4 1.0 copy-done.3
  11.4 0.0 copy-start.4
  11.4 1.0 copy-done.4
  12.3 0.0 copy-start.5
  12.3 1.0 copy-done.5
  13.3 0.0 copy-start.6
  13.3 0.6 copy-done.6
  13.9 97.3 %shard_map.130 = (f32[2,512,512]{2,1,0:T(8,128)}, f32[2,4,256,256]{3,2,1,0:T(8,128)}, f32[2,64,512]{2,1,0:T(8,128)}, f32[2,64,512]{2,1,0:T(8,128)}) custom-call(f32[4,2,256,256]{3,2,1,0:T(8,128)} %copy-done.2, f32[512,512]{1,0:T(8,128)} %copy-done.3, bf16[4,256,512]{2,1,0:T(8,128)(2,1)} %copy-done.4, bf16[512,1024]{1,0:T(8,128)(2,1)} %copy-done.5, ...), custom_call_target="tpu_custom_call" | custom-call | tf_op jit(solution)/shard_map/pallas_call | solution.py:460
  111.2 0.0 copy-start.7
  111.2 3.2 %copy.21 = f32[2,512,512]{2,1,0:T(8,128)} copy(f32[2,512,512]{2,1,0:T(8,128)} %get-tuple-element.18) | data formatting | bytes 4194304
  114.5 0.0 copy-done.7
  114.5 0.0 copy-start.9
  114.5 0.0 copy-start.8
  114.5 1.3 %copy.22 = f32[2,4,256,256]{3,2,1,0:T(8,128)} copy(f32[2,4,256,256]{3,2,1,0:T(8,128)S(1)} %copy-done.7) | data formatting | bytes 4194304
  115.8 0.0 copy-done.9
  115.8 0.7 copy.23
  116.5 0.0 copy-done.8
  116.5 0.7 copy.24
Async XLA Ops:
  2.8 1.6 %copy-start = (f32[2,512,512]{2,1,0:T(8,128)S(1)}, f32[2,512,512]{2,1,0:T(8,128)}, u32[]{:S(2)}) copy-start(f32[2,512,512]{2,1,0:T(8,128)} %obj.3) | copy-start | bytes 6291460
  4.4 1.6 %copy-start.1 = (f32[2,4,256,256]{3,2,1,0:T(8,128)S(1)}, f32[2,4,256,256]{3,2,1,0:T(8,128)}, u32[]{:S(2)}) copy-start(f32[2,4,256,256]{3,2,1,0:T(8,128)} %probe.3) | copy-start | bytes 6291460
  9.1 1.3 %copy-start.2 = (f32[4,2,256,256]{3,2,1,0:T(8,128)}, f32[4,2,256,256]{3,2,1,0:T(8,128)S(1)}, u32[]{:S(2)}) copy-start(f32[4,2,256,256]{3,2,1,0:T(8,128)S(1)} %get-tuple-element.9.patch) | copy-start | bytes 6291460
  10.4 1.0 copy-start.3
  11.4 1.0 copy-start.4
  12.3 1.0 copy-start.5
  13.3 0.6 copy-start.6
  111.2 3.2 %copy-start.7 = (f32[2,4,256,256]{3,2,1,0:T(8,128)S(1)}, f32[2,4,256,256]{3,2,1,0:T(8,128)}, u32[]{:S(2)}) copy-start(f32[2,4,256,256]{3,2,1,0:T(8,128)} %get-tuple-element.19) | copy-start | bytes 6291460
  114.5 1.3 %copy-start.9 = (f32[2,64,512]{2,1,0:T(8,128)S(1)}, f32[2,64,512]{2,1,0:T(8,128)}, u32[]{:S(2)}) copy-start(f32[2,64,512]{2,1,0:T(8,128)} %get-tuple-element.20) | copy-start | bytes 786436
  114.5 2.0 %copy-start.8 = (f32[2,64,512]{2,1,0:T(8,128)S(1)}, f32[2,64,512]{2,1,0:T(8,128)}, u32[]{:S(2)}) copy-start(f32[2,64,512]{2,1,0:T(8,128)} %get-tuple-element.21) | copy-start | bytes 786436
where the time goes:
time: 117 us
  Pallas kernels  100 us (85%)
  local copies, waits for them, and re-layouts  15.5 us (13%)
  between operations  1.32 us (1%)
    pallas_call x1, Pallas kernels, local(): pl.pallas_call(kernel, out_shape=(shape(2, TILE, TILE), shape(2, MODES, P...  97.3 us
    unnamed x26, local copies, waits for them, and re-layouts  15.5 us
    pallas_call x1, Pallas kernels, local(): pl.pallas_call(prepare, out_shape=(shape(NPAT, 2, PAT, PAT), shape(TILE,...  3.1 us

commit v1 on v0

v1 whole, which is shorter than its diff:
```python
import numpy as np
import jax
import jax.numpy as jnp
import ml_dtypes
from jax import lax
from jax.experimental import pallas as pl
from jax.experimental.pallas import tpu as pltpu
from jax.sharding import PartitionSpec as P

F32, BF16 = jnp.float32, jnp.bfloat16
MESH = pl.DeviceIdType.MESH
PAT, TILE, MODES, NPAT, HALF = 256, 512, 4, 4, 128
EDGE, BLOCK, NPIECE, KP = 64, 128, 4, 2
LIMIT = 44
SUMS = MODES + 1


def tables():
    n = np.arange(HALF)[:, None]
    out = []
    for p in range(2):
        k = 2 * np.arange(HALF)[None, :] + p
        angle = 2 * np.pi * ((n * k) % PAT) / PAT
        c, s = np.cos(angle) / 16.0, np.sin(angle) / 16.0
        full = np.block([[c, -s], [s, c]])
        out.append(full)
    full = np.stack([np.stack(out), np.stack([o.T for o in out])]).astype(np.float32)
    hi = full.astype(ml_dtypes.bfloat16)
    lo = (full - hi.astype(np.float32)).astype(ml_dtypes.bfloat16)
    perm = np.zeros((PAT, PAT), np.float32)
    for j in range(PAT):
        perm[2 * (j % HALF) + j // HALF, j] = 1.0
    return np.stack([hi, lo], axis=2), np.stack([perm, perm.T]).astype(ml_dtypes.bfloat16)


def dot(a, b):
    return jnp.dot(a, b, preferred_element_type=F32)


def split(a):
    h = a.astype(BF16)
    return h, (a - h.astype(F32)).astype(BF16)


def right(a, t, d, p):
    h, l = split(a)
    return dot(h, t[d, p, 1]) + dot(h, t[d, p, 0]) + dot(l, t[d, p, 0])


def left(t, d, p, a):
    h, l = split(a)
    return dot(t[d, p, 0], l) + dot(t[d, p, 1], h) + dot(t[d, p, 0], h)


def along(shape, axis):
    return lax.broadcasted_iota(jnp.int32, shape, axis)


def lane_turn(block, by):
    return pltpu.roll(block, by & (HALF - 1), 1)


def row_turn(block, by):
    return pltpu.roll(block, by & 7, 1)


def window(obj, plane, row, col):
    base = pl.multiple_of(jnp.minimum((row >> 3) << 3, TILE - PAT - 8), 8)
    side = pl.multiple_of(jnp.minimum((col >> 7) << 7, TILE - PAT - HALF), HALF)
    down, right_by = row - base, col - side
    block = obj[plane, pl.ds(base, PAT + 8), pl.ds(side, PAT + HALF)]
    block = block.reshape((PAT + 8) // 8, 8, PAT + HALF)
    turned = row_turn(block, 8 - down)
    keep = along((PAT // 8, 8, PAT + HALF), 1) + down < 8
    block = jnp.where(keep, turned[:-1], turned[1:]).reshape(PAT, PAT + HALF)
    parts = [lane_turn(block[:, t * HALF:(t + 1) * HALF], HALF - right_by) for t in range(3)]
    keep = along((PAT, HALF), 1) + right_by < HALF
    return jnp.concatenate([jnp.where(keep, parts[t], parts[t + 1]) for t in range(2)], axis=1)


def prepare(pos, pieces, live, obj_far, patch, shifts, mask, denom, obj, sems):
    copies = []
    for i in range(4):
        rows = (i // 2, pl.ds((i % 2) * PAT, PAT))
        copies.append(pltpu.make_async_copy(obj_far.at[rows], obj.at[rows], sems.at[i]))
        copies[-1].start()
    for j in range(NPAT):
        shifts[j:j + 1, :] = jnp.full((1, TILE), pos[0, j], jnp.int32)
        shifts[NPAT + j:NPAT + j + 1, :] = jnp.full((1, TILE), pos[1, j], jnp.int32)
    first, second, count = pieces[0, 0], pieces[0, 1], live[0, 0]
    has_lower = lax.axis_index("region") < 31
    mask[...] = jnp.zeros_like(mask)
    for b in range(NPIECE):
        active = (((first == b) & (count > 0)) | ((second == b) & (count > 1))) & has_lower
        for i, chosen in enumerate((first == b, second == b, active)):
            value = jnp.where(chosen, 1.0, 0.0).astype(F32)
            mask[i:i + 1, b * BLOCK:(b + 1) * BLOCK] = jnp.full((1, BLOCK), value, F32)
    for copy in copies:
        copy.wait()
    total = jnp.zeros((PAT, PAT), F32)
    for j in range(NPAT):
        pr, pi = window(obj, 0, pos[0, j], pos[1, j]), window(obj, 1, pos[0, j], pos[1, j])
        patch[j, 0] = pr
        patch[j, 1] = pi
        total = total + pr * pr + pi * pi
    denom[...] = total


class Place:
    def __init__(self):
        self.group, self.region = lax.axis_index("group"), lax.axis_index("region")
        core, y_lo = lax.rem(self.group, 2), self.group // 2
        x, z, y_hi = self.region // 8, lax.rem(self.region // 2, 4), lax.rem(self.region, 2)
        y = y_hi * 2 + y_lo
        self.core = core
        self.v, self.u, self.w = x + core * (z - x), y + core * (x - y), z + core * (y - z)
        self.number = self.u * 4 + self.w

    def at(self, v, u, w):
        core = self.core
        x, y, z = v + core * (u - v), u + core * (w - u), w + core * (v - w)
        return (lax.rem(y, 2) * 2 + core, (x * 4 + z) * 2 + y // 2)

    def sibling(self):
        return (self.group + 1 - 2 * self.core, self.region)

    def on_line(self, k):
        v = lax.rem(self.v + k, 4)
        return self.at(v, self.u, self.w), v

    def in_plane(self, k):
        u, w = lax.rem(self.u + k // 4, 4), lax.rem(self.w + lax.rem(k, 4), 4)
        return self.at(self.v, u, w), u * 4 + w

    def region_by(self, by):
        return (self.group, lax.rem(self.region + 32 + by, 32))


def send(src, dst, sems, index, device):
    copy = pltpu.make_async_remote_copy(
        src_ref=src, dst_ref=dst, send_sem=sems[0].at[index], recv_sem=sems[1].at[index], device_id=device, device_id_type=MESH
    )
    copy.start()


def await_bytes(ref, sem):
    pltpu.make_async_copy(ref, ref, sem).wait()


def packed(block, hot):
    out = []
    for slot in range(KP):
        chosen = block[:, :BLOCK]
        for b in range(1, NPIECE):
            flag = jnp.broadcast_to(hot[slot:slot + 1, b * BLOCK:(b + 1) * BLOCK], chosen.shape)
            chosen = jnp.where(flag > 0.5, block[:, b * BLOCK:(b + 1) * BLOCK], chosen)
        out.append(chosen)
    return jnp.concatenate(out, axis=1)


def unpacked(block, hot):
    flag = jnp.broadcast_to(hot[0:1, :], (block.shape[0], TILE)) > 0.5
    first = jnp.concatenate([block[:, :BLOCK]] * NPIECE, axis=1)
    second = jnp.concatenate([block[:, BLOCK:]] * NPIECE, axis=1)
    return jnp.where(flag, first, second)


def kernel(
    patch, shifts, mask, denom, probe, tab, far_obj, far_amp, far_perm, far_top, far_bottom,
    mid, probe_out, top_out, bottom_out,
    far, factor, grad, spread_hi, spread_lo, numer,
    from_core, part, from_line, block, from_plane, tiles, fresh, scale,
    obj, amp, perm, dual_top, dual_bottom, mask_in, up, low, up_sent, low_sent, from_below, from_above,
    core_send, core_recv, line_send, line_recv, plane_send, plane_recv,
    back_plane_send, back_plane_recv, back_line_send, back_line_recv, back_core_send, back_core_recv,
    edge_send, edge_recv, load_sem,
):
    loads = [
        pltpu.make_async_copy(source, target, load_sem.at[i])
        for i, (source, target) in enumerate(
            ((far_perm, perm), (far_amp, amp), (far_obj, obj), (far_top, dual_top), (far_bottom, dual_bottom))
        )
    ]
    for load in loads:
        load.start()
    me = Place()
    barrier = pltpu.get_barrier_semaphore()

    def greet(device):
        pl.semaphore_signal(barrier, inc=1, device_id=device, device_id_type=MESH)

    greet(me.sibling())
    for k in range(1, 4):
        greet(me.on_line(k)[0])
    for k in range(1, 16):
        greet(me.in_plane(k)[0])
    greet(me.region_by(1))
    greet(me.region_by(-1))

    grad[...] = jnp.zeros_like(grad)

    def forward(j, _):
        pr, pi = patch[j, 0], patch[j, 1]

        def mode(m, _):
            pr, pi = patch[j, 0], patch[j, 1]
            qr, qi = probe[0, m], probe[1, m]
            er = qr * pr - qi * pi
            ei = qr * pi + qi * pr
            lo = jnp.concatenate([er[:, :HALF], ei[:, :HALF]], axis=1)
            hi = jnp.concatenate([er[:, HALF:], ei[:, HALF:]], axis=1)
            y0 = right(lo + hi, tab, 0, 0)
            y1 = right(lo - hi, tab, 0, 1)
            yr = jnp.concatenate([y0[:, :HALF], y1[:, :HALF]], axis=1)
            yi = jnp.concatenate([y0[:, HALF:], y1[:, HALF:]], axis=1)
            top = jnp.concatenate([yr[:HALF], yi[:HALF]], axis=0)
            bot = jnp.concatenate([yr[HALF:], yi[HALF:]], axis=0)
            far[m * NPAT + j, 0] = left(tab, 1, 0, top + bot)
            far[m * NPAT + j, 1] = left(tab, 1, 1, top - bot)
            return 0

        lax.fori_loop(0, MODES, mode, 0, unroll=True)
        h, l = split(amp[j])
        h, l = split(dot(h, perm[0]) + dot(l, perm[0]))
        full = dot(perm[1], h) + dot(perm[1], l)
        for q in range(2):
            power = jnp.zeros((HALF, PAT), F32)
            for m in range(MODES):
                z = far[m * NPAT + j, q]
                power = power + z[:HALF] * z[:HALF] + z[HALF:] * z[HALF:]
            f = full[q * HALF:(q + 1) * HALF] / jnp.maximum(jnp.sqrt(power), 0.5)
            factor[j, q, :HALF] = f
            factor[j, q, HALF:] = f
        return 0

    def inverse(m, first, last):
        def one(j, _):
            g0 = left(tab, 0, 0, far[m * NPAT + j, 0] * factor[j, 0])
            g1 = left(tab, 0, 1, far[m * NPAT + j, 1] * factor[j, 1])
            top, bot = g0 + g1, g0 - g1
            xr = jnp.concatenate([top[:HALF], bot[:HALF]], axis=0)
            xi = jnp.concatenate([top[HALF:], bot[HALF:]], axis=0)
            b0 = right(jnp.concatenate([xr[:, :HALF], xi[:, :HALF]], axis=1), tab, 1, 0)
            b1 = right(jnp.concatenate([xr[:, HALF:], xi[:, HALF:]], axis=1), tab, 1, 1)
            lo, hi = b0 + b1, b0 - b1
            br = jnp.concatenate([lo[:, :HALF], hi[:, :HALF]], axis=1)
            bi = jnp.concatenate([lo[:, HALF:], hi[:, HALF:]], axis=1)
            qr, qi = probe[0, m], probe[1, m]
            grad[j, 0] += qr * br + qi * bi
            grad[j, 1] += qr * bi - qi * br
            pr, pi = patch[j, 0], patch[j, 1]
            numer[0, m] += pr * br + pi * bi
            numer[1, m] += pr * bi - pi * br
            return 0

        if first == 0:
            numer[0, m] = jnp.zeros((PAT, PAT), F32)
            numer[1, m] = jnp.zeros((PAT, PAT), F32)
        lax.fori_loop(first, last, one, 0, unroll=True)

    line_rows = pl.ds(pl.multiple_of(me.v * 64, 64), 64)
    core_sems, line_sems, plane_sems = (core_send, core_recv), (line_send, line_recv), (plane_send, plane_recv)
    back_plane_sems, back_line_sems = (back_plane_send, back_plane_recv), (back_line_send, back_line_recv)
    back_core_sems, edge_sems = (back_core_send, back_core_recv), (edge_send, edge_recv)

    def mine(m):
        return denom[...] if m == MODES else numer[me.core, m]

    def core_start(m):
        send(denom if m == MODES else numer.at[1 - me.core, m], from_core.at[m], core_sems, m, me.sibling())

    def line_start(m):
        await_bytes(from_core.at[m], core_recv.at[m])
        part[m] = mine(m) + from_core[m]
        for k in range(1, 4):
            device, there = me.on_line(k)
            source = part.at[m, pl.ds(pl.multiple_of(there * 64, 64), 64), :]
            send(source, from_line.at[m, k - 1], line_sems, m, device)

    def plane_start(m):
        await_bytes(from_line.at[m], line_recv.at[m])
        total = part[m, line_rows, :] + from_line[m, 0] + from_line[m, 1] + from_line[m, 2]
        for k in range(16):
            block[m, k] = total[(k // 2) * 8:(k // 2) * 8 + 8, (k % 2) * HALF:(k % 2 + 1) * HALF]

        for k in range(1, 16):
            device, there = me.in_plane(k)
            send(block.at[m, there], from_plane.at[m, k - 1], plane_sems, m, device)

    def total_of(m):
        await_bytes(from_plane.at[m], plane_recv.at[m])
        total = block[m, me.number]
        for k in range(15):
            total = total + from_plane[m, k]
        return total

    def denom_end():
        scale[...] = total_of(MODES) + 1.0

    def back_start(m):
        row = pl.multiple_of(me.v * 64 + (me.number // 2) * 8, 8)
        column = pl.multiple_of(lax.rem(me.number, 2) * HALF, HALF)
        old = probe[me.core, m, pl.ds(row, 8), pl.ds(column, HALF)]
        tiles[m, me.number] = (old + total_of(m)) / scale[...]
        own = tiles.at[m, me.number]

        for k in range(1, 16):
            send(own, own, back_plane_sems, m, me.in_plane(k)[0])

    def back_line_start(m):
        await_bytes(tiles.at[m, pl.ds(0, 15)], back_plane_recv.at[m])
        rows = [jnp.concatenate([tiles[m, 2 * i], tiles[m, 2 * i + 1]], axis=1) for i in range(8)]
        fresh[me.core, m, line_rows, :] = jnp.concatenate(rows, axis=0)
        own = fresh.at[me.core, m, line_rows, :]
        for k in range(1, 4):
            send(own, own, back_line_sems, m, me.on_line(k)[0])

    def back_core_start(m):
        await_bytes(fresh.at[me.core, m, pl.ds(0, 192), :], back_line_recv.at[m])
        send(fresh.at[me.core, m], fresh.at[me.core, m], back_core_sems, m, me.sibling())

    def back_end(m):
        await_bytes(fresh.at[1 - me.core, m], back_core_recv.at[m])
        for plane in range(2):
            probe_out[plane, m] = fresh[plane, m]

    def spread_plane(plane, j, block):
        rows = pl.ds(pl.multiple_of(j * PAT, PAT), PAT)
        by = jnp.broadcast_to(shifts[pl.ds(NPAT + j, 1), :], (PAT, TILE))
        columns = jnp.where(along((PAT, TILE), 1) - along((PAT, TILE), 0) == by, 1.0, 0.0).astype(BF16)
        h, l = split(block)
        h, l = split(dot(h, columns) + dot(l, columns))
        spread_hi[plane, rows, :] = h
        spread_lo[plane, rows, :] = l

    def spread(first, last):
        def one(j, _):
            spread_plane(0, j, grad[j, 0])
            spread_plane(1, j, grad[j, 1])
            return 0

        lax.fori_loop(first, last, one, 0, unroll=True)

    def spread_weights():
        power = sum(probe[0, m] * probe[0, m] + probe[1, m] * probe[1, m] for m in range(MODES))
        for j in range(NPAT):
            spread_plane(2, j, power)

    def update(starts, count):
        chosen = []
        for j in range(NPAT):
            by = jnp.broadcast_to(shifts[j:j + 1, :PAT], (count, PAT))
            away = along((count, PAT), 0) - along((count, PAT), 1)
            chosen.append(jnp.concatenate([jnp.where(away + start == by, 1.0, 0.0).astype(BF16) for start in starts], axis=0))
        chosen = jnp.concatenate(chosen, axis=1)
        sums = [dot(chosen, spread_hi[plane]) + dot(chosen, spread_lo[plane]) for plane in range(3)]
        for i, start in enumerate(starts):
            rows, here = slice(start, start + count), slice(i * count, (i + 1) * count)
            inverse_weight = 1.0 / (sums[2][here] + 1.0)
            for plane in range(2):
                mid[plane, rows, :] = (obj[plane, rows, :] + sums[plane][here]) * inverse_weight

    def mask_start():
        send(mask, mask_in, edge_sems, 0, me.region_by(1))

    def edge_start():
        await_bytes(mask_in, edge_recv.at[0])
        for plane in range(2):
            up[plane] = mid[plane, :EDGE] + dual_top[plane]
            low[plane] = mid[plane, TILE - EDGE:] + dual_bottom[plane]
            up_sent[plane] = packed(up[plane], mask_in)
            low_sent[plane] = packed(low[plane], mask)
        send(up_sent, from_below, edge_sems, 1, me.region_by(-1))
        send(low_sent, from_above, edge_sems, 2, me.region_by(1))

    def edge_end():
        await_bytes(from_below, edge_recv.at[1])
        await_bytes(from_above, edge_recv.at[2])
        for plane in range(2):
            here = mid[plane, TILE - EDGE:]
            agreed = 0.5 * (low[plane] + unpacked(from_below[plane], mask))
            active = jnp.broadcast_to(mask[2:3, :], (EDGE, TILE)) > 0.5
            bottom_out[plane] = jnp.where(active, dual_bottom[plane] + (here - agreed), dual_bottom[plane])
            mid[plane, TILE - EDGE:] = jnp.where(active, agreed, here)
            here = mid[plane, :EDGE]
            agreed = 0.5 * (unpacked(from_above[plane], mask_in) + up[plane])
            active = jnp.broadcast_to(mask_in[2:3, :], (EDGE, TILE)) > 0.5
            top_out[plane] = jnp.where(active, dual_top[plane] + (here - agreed), dual_top[plane])
            mid[plane, :EDGE] = jnp.where(active, agreed, here)

    loads[0].wait()
    loads[1].wait()
    lax.fori_loop(0, 1, forward, 0)
    lax.fori_loop(1, 2, forward, 0)
    lax.fori_loop(2, 3, forward, 0)
    pl.semaphore_wait(barrier, 21)
    mask_start()
    core_start(MODES)
    lax.fori_loop(3, 4, forward, 0)
    line_start(MODES)
    inverse(0, 0, 4)
    core_start(0)
    inverse(1, 0, 2)
    line_start(0)
    plane_start(MODES)
    inverse(1, 2, 4)
    core_start(1)
    inverse(2, 0, 2)
    line_start(1)
    inverse(2, 2, 4)
    core_start(2)
    plane_start(0)
    inverse(3, 0, 2)
    line_start(2)
    inverse(3, 2, 4)
    core_start(3)
    denom_end()
    spread(0, 2)
    plane_start(1)
    spread(2, 4)
    line_start(3)
    back_start(0)
    spread_weights()
    plane_start(2)
    for load in loads[2:]:
        load.wait()
    update((0, TILE - EDGE), EDGE)
    edge_start()
    back_start(1)
    update((EDGE,), TILE // 2 - EDGE)
    plane_start(3)
    update((TILE // 2,), TILE // 2 - EDGE)
    back_line_start(0)
    back_start(2)
    back_line_start(1)
    back_start(3)
    back_core_start(0)
    back_line_start(2)
    edge_end()
    back_end(0)
    back_core_start(1)
    back_line_start(3)
    back_end(1)
    back_core_start(2)
    back_end(2)
    back_core_start(3)
    back_end(3)

    for m in range(SUMS):
        await_bytes(from_core.at[m], core_send.at[m])
        await_bytes(from_line.at[m], line_send.at[m])
        await_bytes(from_plane.at[m], plane_send.at[m])
    for m in range(MODES):
        await_bytes(tiles.at[m, pl.ds(0, 15)], back_plane_send.at[m])
        await_bytes(fresh.at[0, m, pl.ds(0, 192), :], back_line_send.at[m])
        await_bytes(fresh.at[0, m], back_core_send.at[m])
    await_bytes(mask_in, edge_send.at[0])
    await_bytes(up_sent, edge_send.at[1])
    await_bytes(low_sent, edge_send.at[2])


def local(object_field, probe, amplitudes, positions, dual_top, dual_bottom, pieces, live):
    tab, perm = tables()
    vmem = pl.BlockSpec(memory_space=pltpu.VMEM)
    smem = pl.BlockSpec(memory_space=pltpu.SMEM)
    far = pl.BlockSpec(memory_space=pl.ANY)
    buf = lambda *shape: pltpu.VMEM(shape, F32)
    half = lambda *shape: pltpu.VMEM(shape, BF16)
    dma = lambda *shape: pltpu.SemaphoreType.DMA(shape)
    edge, sent = (2, EDGE, TILE), (2, EDGE, KP * BLOCK)
    shape = lambda *dims: jax.ShapeDtypeStruct(dims, F32)
    prepared = pl.pallas_call(
        prepare,
        out_shape=(shape(NPAT, 2, PAT, PAT), jax.ShapeDtypeStruct((2 * NPAT, TILE), jnp.int32), shape(8, TILE), shape(PAT, PAT)),
        in_specs=[smem] * 3 + [far],
        out_specs=(vmem,) * 4,
        scratch_shapes=[buf(2, TILE, TILE), dma(4)],
        compiler_params=pltpu.CompilerParams(vmem_limit_bytes=16 * 1024 * 1024),
    )(positions.T, pieces.T, live, object_field)
    return pl.pallas_call(
        kernel,
        out_shape=(shape(2, TILE, TILE), shape(2, MODES, PAT, PAT), shape(*edge), shape(*edge)),
        in_specs=[vmem] * 6 + [far] * 5,
        out_specs=(vmem,) * 4,
        scratch_shapes=[
            buf(MODES * NPAT, 2, PAT, PAT), buf(NPAT, 2, PAT, PAT), buf(NPAT, 2, PAT, PAT),
            half(3, NPAT * PAT, TILE), half(3, NPAT * PAT, TILE), buf(2, MODES, PAT, PAT),
            buf(SUMS, PAT, PAT), buf(SUMS, PAT, PAT), buf(SUMS, 3, 64, PAT), buf(SUMS, 16, 8, HALF), buf(SUMS, 15, 8, HALF),
            buf(MODES, 16, 8, HALF), buf(2, MODES, PAT, PAT), buf(8, HALF),
            buf(2, TILE, TILE), buf(NPAT, PAT, PAT), half(2, PAT, PAT), buf(*edge), buf(*edge),
            buf(8, TILE), buf(*edge), buf(*edge), buf(*sent), buf(*sent), buf(*sent), buf(*sent),
        ] + [dma(SUMS)] * 6 + [dma(MODES)] * 6 + [dma(3), dma(3), dma(5)],
        compiler_params=pltpu.CompilerParams(vmem_limit_bytes=LIMIT * 1024 * 1024, collective_id=0, has_side_effects=True),
    )(*prepared, probe, jnp.asarray(tab), object_field, amplitudes, jnp.asarray(perm), dual_top, dual_bottom)


def solution(mesh):
    tiles = P(None, "region", "group")
    return jax.shard_map(
        local,
        mesh=mesh,
        in_specs=(tiles, P(), P("region", "group", None), P("region", "group"), tiles, tiles, P("region", "group"), P("region", "group")),
        out_specs=(tiles, P(), tiles, tiles),
        check_vma=False,
    )
```

time: 117 us -> 71.3 us (0.61)
  Pallas kernels: 100 us -> 59.9 us
  local copies, waits for them, and re-layouts: 15.5 us -> 9.82 us
    pallas_call x1, Pallas kernels: 97.3 us -> 58.2 us  [local(): pl.pallas_call(kernel, out_shape=(shape(2, TILE, TILE), shape(2, MODES, P...]
    unnamed x26 -> x20, local copies, waits for them, and re-layouts: 15.5 us -> 9.82 us
    pallas_call x1, Pallas kernels: 3.1 us -> 1.65 us  [local(): pl.pallas_call(prepare, out_shape=(shape(NPAT, 2, PAT, PAT), jax.ShapeDty...]
where the time goes in v1:
time: 71.3 us; the launch traced here: 71 us
  Pallas kernels  59.9 us (84%)
  local copies, waits for them, and re-layouts  9.82 us (14%)
  between operations  1.33 us (2%)
    pallas_call x1, Pallas kernels, local(): pl.pallas_call(kernel, out_shape=(shape(2, TILE, TILE), shape(2, MODES, P...  58.2 us
    unnamed x20, local copies, waits for them, and re-layouts  9.82 us
    pallas_call x1, Pallas kernels, local(): pl.pallas_call(prepare, out_shape=(shape(NPAT, 2, PAT, PAT), jax.ShapeDty...  1.65 us

profile of v1, /device:TPU:1, one launch (start us, length us, event | category | flops | bytes accessed | tf_op | source)
XLA Modules:
  0.0 71.0 jit_solution(41029997022126708)
XLA Ops:
  1.3 0.0 copy-start
  1.3 1.6 %copy-done = f32[2,512,512]{2,1,0:T(8,128)S(1)} copy-done((f32[2,512,512]{2,1,0:T(8,128)S(1)}, f32[2,512,512]{2,1,0:T(8,128)}, u32[]{:S(2)}) %copy-start) | copy-done | bytes 2097176
  2.9 0.0 copy-start.6
  2.9 0.7 copy-done.6
  3.6 0.0 copy-start.7
  3.6 0.7 copy-done.7
  4.2 0.0 copy-start.1
  4.2 0.0 copy-start.2
  4.2 1.7 %shard_map.129 = (f32[4,2,256,256]{3,2,1,0:T(8,128)S(1)}, s32[8,512]{1,0:T(8,128)S(1)}, f32[8,512]{1,0:T(8,128)S(1)}, f32[256,256]{1,0:T(8,128)S(1)}) custom-call(s32[2,4]{1,0:T(2,128)S(1)} %bitcast.2, s32[1,2]{1,0:T(1,128)S(1)} %bitcast.3, s32[1,1]{1,0:T(1,128)S(6)} %copy.18.live, f32[2,512,512]{2,1,0:T(8,128)S(1)} %copy-done), custom_call_target="tpu_custom_call" | custom-call | tf_op jit(solution)/shard_map/pallas_call | solution.py:472
  5.9 0.0 copy-done.1
  5.9 0.0 copy-done.2
  5.9 0.0 copy-start.3
  5.9 0.9 %copy-done.3 = f32[2,64,512]{2,1,0:T(8,128)S(1)} copy-done((f32[2,64,512]{2,1,0:T(8,128)S(1)}, f32[2,64,512]{2,1,0:T(8,128)}, u32[]{:S(2)}) %copy-start.3) | copy-done | bytes 262168
  6.8 0.0 copy-start.4
  6.9 0.9 %copy-done.4 = f32[2,64,512]{2,1,0:T(8,128)S(1)} copy-done((f32[2,64,512]{2,1,0:T(8,128)S(1)}, f32[2,64,512]{2,1,0:T(8,128)}, u32[]{:S(2)}) %copy-start.4) | copy-done | bytes 262168
  7.8 0.0 copy-start.5
  7.8 0.9 %copy-done.5 = bf16[2,256,256]{2,1,0:T(8,128)(2,1)S(1)} copy-done((bf16[2,256,256]{2,1,0:T(8,128)(2,1)S(1)}, bf16[2,256,256]{2,1,0:T(8,128)(2,1)}, u32[]{:S(2)}) %copy-start.5) | copy-done | bytes 262168
  8.7 58.2 %shard_map.130 = (f32[2,512,512]{2,1,0:T(8,128)S(1)}, f32[2,4,256,256]{3,2,1,0:T(8,128)S(1)}, f32[2,64,512]{2,1,0:T(8,128)S(1)}, f32[2,64,512]{2,1,0:T(8,128)S(1)}) custom-call(f32[4,2,256,256]{3,2,1,0:T(8,128)S(1)} %get-tuple-element.8.patch, s32[8,512]{1,0:T(8,128)S(1)} %get-tuple-element.9.shifts, f32[8,512]{1,0:T(8,128)S(1)} %get-tuple-element.10.mask, ...), custom_call_target="tpu_custom_call" | custom-call | tf_op jit(solution)/shard_map/pallas_call | solution.py:480
  67.0 1.3 %copy.19 = f32[2,512,512]{2,1,0:T(8,128)} copy(f32[2,512,512]{2,1,0:T(8,128)S(1)} %get-tuple-element.16) | data formatting | bytes 4194304
  68.3 1.3 %copy.20 = f32[2,4,256,256]{3,2,1,0:T(8,128)} copy(f32[2,4,256,256]{3,2,1,0:T(8,128)S(1)} %get-tuple-element.17) | data formatting | bytes 4194304
  69.6 0.7 copy.21
  70.3 0.7 copy.22
Async XLA Ops:
  1.3 1.6 %copy-start = (f32[2,512,512]{2,1,0:T(8,128)S(1)}, f32[2,512,512]{2,1,0:T(8,128)}, u32[]{:S(2)}) copy-start(f32[2,512,512]{2,1,0:T(8,128)} %far_obj.1) | copy-start | bytes 6291460
  2.9 0.7 copy-start.6
  3.6 0.7 copy-start.7
  4.2 1.7 %copy-start.1 = (f32[4,256,256]{2,1,0:T(8,128)S(1)}, f32[4,256,256]{2,1,0:T(8,128)}, u32[]{:S(2)}) copy-start(f32[4,256,256]{2,1,0:T(8,128)} %far_amp.1) | copy-start | bytes 3145732
  4.2 1.7 %copy-start.2 = (bf16[2,2,2,256,256]{4,3,2,1,0:T(8,128)(2,1)S(1)}, bf16[2,2,2,256,256]{4,3,2,1,0:T(8,128)(2,1)}, u32[]{:S(2)}) copy-start(bf16[2,2,2,256,256]{4,3,2,1,0:T(8,128)(2,1)} %constant.4.clone.tab) | copy-start | bytes 3145732
  5.9 1.0 %copy-start.3 = (f32[2,64,512]{2,1,0:T(8,128)S(1)}, f32[2,64,512]{2,1,0:T(8,128)}, u32[]{:S(2)}) copy-start(f32[2,64,512]{2,1,0:T(8,128)} %far_top.1) | copy-start | bytes 786436
  6.8 0.9 %copy-start.4 = (f32[2,64,512]{2,1,0:T(8,128)S(1)}, f32[2,64,512]{2,1,0:T(8,128)}, u32[]{:S(2)}) copy-start(f32[2,64,512]{2,1,0:T(8,128)} %far_bottom.1) | copy-start | bytes 786436
  7.8 0.9 %copy-start.5 = (bf16[2,256,256]{2,1,0:T(8,128)(2,1)S(1)}, bf16[2,256,256]{2,1,0:T(8,128)(2,1)}, u32[]{:S(2)}) copy-start(bf16[2,256,256]{2,1,0:T(8,128)(2,1)} %constant.5.clone.far_perm) | copy-start | bytes 786436

commit v2 on v1

--- a/solution.py
+++ b/solution.py
@@ -11,7 +11,9 @@
 MESH = pl.DeviceIdType.MESH
 PAT, TILE, MODES, NPAT, HALF = 256, 512, 4, 4, 128
 EDGE, BLOCK, NPIECE, KP = 64, 128, 4, 2
-LIMIT = 44
+LOADS = 21
+LIMIT = 46
+POWER, DUALS = NPAT * PAT, (NPAT + 1) * PAT
 SUMS = MODES + 1
 
 
@@ -27,10 +29,7 @@
     full = np.stack([np.stack(out), np.stack([o.T for o in out])]).astype(np.float32)
     hi = full.astype(ml_dtypes.bfloat16)
     lo = (full - hi.astype(np.float32)).astype(ml_dtypes.bfloat16)
-    perm = np.zeros((PAT, PAT), np.float32)
-    for j in range(PAT):
-        perm[2 * (j % HALF) + j // HALF, j] = 1.0
-    return np.stack([hi, lo], axis=2), np.stack([perm, perm.T]).astype(ml_dtypes.bfloat16)
+    return np.stack([hi, lo], axis=2)
 
 
 def dot(a, b):
@@ -78,32 +77,37 @@
     return jnp.concatenate([jnp.where(keep, parts[t], parts[t + 1]) for t in range(2)], axis=1)
 
 
-def prepare(pos, pieces, live, obj_far, patch, shifts, mask, denom, obj, sems):
-    copies = []
+def prepare(pos, far_obj, far_top, far_bottom, work_out, work, obj, sems):
+    loads, stores = [], []
     for i in range(4):
         rows = (i // 2, pl.ds((i % 2) * PAT, PAT))
-        copies.append(pltpu.make_async_copy(obj_far.at[rows], obj.at[rows], sems.at[i]))
-        copies[-1].start()
+        loads.append(pltpu.make_async_copy(far_obj.at[rows], obj.at[rows], sems.at[i]))
+    for i, source in enumerate((far_top.at[0], far_top.at[1], far_bottom.at[0], far_bottom.at[1])):
+        loads.append(pltpu.make_async_copy(source, work.at[pl.ds(DUALS + i * EDGE, EDGE)], sems.at[4 + i]))
+    for copy in loads:
+        copy.start()
     for j in range(NPAT):
-        shifts[j:j + 1, :] = jnp.full((1, TILE), pos[0, j], jnp.int32)
-        shifts[NPAT + j:NPAT + j + 1, :] = jnp.full((1, TILE), pos[1, j], jnp.int32)
-    first, second, count = pieces[0, 0], pieces[0, 1], live[0, 0]
-    has_lower = lax.axis_index("region") < 31
-    mask[...] = jnp.zeros_like(mask)
-    for b in range(NPIECE):
-        active = (((first == b) & (count > 0)) | ((second == b) & (count > 1))) & has_lower
-        for i, chosen in enumerate((first == b, second == b, active)):
-            value = jnp.where(chosen, 1.0, 0.0).astype(F32)
-            mask[i:i + 1, b * BLOCK:(b + 1) * BLOCK] = jnp.full((1, BLOCK), value, F32)
-    for copy in copies:
+        work[POWER + j:POWER + j + 1, PAT:] = jnp.full((1, PAT), pos[0, j].astype(F32), F32)
+        work[POWER + NPAT + j:POWER + NPAT + j + 1, PAT:] = jnp.full((1, PAT), pos[1, j].astype(F32), F32)
+    for copy in loads[:4]:
         copy.wait()
     total = jnp.zeros((PAT, PAT), F32)
     for j in range(NPAT):
         pr, pi = window(obj, 0, pos[0, j], pos[1, j]), window(obj, 1, pos[0, j], pos[1, j])
-        patch[j, 0] = pr
-        patch[j, 1] = pi
+        rows = pl.ds(j * PAT, PAT)
+        work[rows, :PAT] = pr
+        work[rows, PAT:] = pi
+        stores.append(pltpu.make_async_copy(work.at[rows], work_out.at[rows], sems.at[8 + j]))
+        stores[-1].start()
         total = total + pr * pr + pi * pi
-    denom[...] = total
+    work[POWER:POWER + PAT, :PAT] = total
+    for copy in loads[4:]:
+        copy.wait()
+    rows = pl.ds(POWER, 2 * PAT)
+    stores.append(pltpu.make_async_copy(work.at[rows], work_out.at[rows], sems.at[12]))
+    stores[-1].start()
+    for copy in stores:
+        copy.wait()
 
 
 class Place:
@@ -166,23 +170,26 @@
 
 
 def kernel(
-    patch, shifts, mask, denom, probe, tab, far_obj, far_amp, far_perm, far_top, far_bottom,
+    far_work, far_probe, far_tab, pieces, live, far_obj, far_amp,
     mid, probe_out, top_out, bottom_out,
     far, factor, grad, spread_hi, spread_lo, numer,
     from_core, part, from_line, block, from_plane, tiles, fresh, scale,
-    obj, amp, perm, dual_top, dual_bottom, mask_in, up, low, up_sent, low_sent, from_below, from_above,
+    work, denom, probe, tab, obj, amp, perm, mask, mask_in, up, low, up_sent, low_sent, from_below, from_above,
     core_send, core_recv, line_send, line_recv, plane_send, plane_recv,
     back_plane_send, back_plane_recv, back_line_send, back_line_recv, back_core_send, back_core_recv,
     edge_send, edge_recv, load_sem,
 ):
-    loads = [
-        pltpu.make_async_copy(source, target, load_sem.at[i])
-        for i, (source, target) in enumerate(
-            ((far_perm, perm), (far_amp, amp), (far_obj, obj), (far_top, dual_top), (far_bottom, dual_bottom))
-        )
-    ]
+    pairs = [(far_work.at[pl.ds(j * PAT, PAT)], work.at[pl.ds(j * PAT, PAT)]) for j in range(NPAT + 2)]
+    pairs = [(far_tab, tab)] + [(far_probe.at[plane, m], probe.at[plane, m]) for m in range(MODES) for plane in range(2)] + pairs
+    pairs += [(far_amp.at[j], amp.at[j]) for j in range(NPAT)] + [(far_obj.at[plane], obj.at[plane]) for plane in range(2)]
+    loads = [pltpu.make_async_copy(source, target, load_sem.at[i]) for i, (source, target) in enumerate(pairs)]
     for load in loads:
         load.start()
+
+    def wait_loads(first, last):
+        for load in loads[first:last]:
+            load.wait()
+
     me = Place()
     barrier = pltpu.get_barrier_semaphore()
 
@@ -197,13 +204,21 @@
     greet(me.region_by(1))
     greet(me.region_by(-1))
 
+    for i, (axis, other) in enumerate(((1, 0), (0, 1))):
+        place = along((PAT, PAT), axis)
+        source = 2 * (place & (HALF - 1)) + (place >> 7)
+        perm[i] = jnp.where(along((PAT, PAT), other) == source, 1.0, 0.0).astype(BF16)
     grad[...] = jnp.zeros_like(grad)
 
+    def window_of(j):
+        rows = pl.ds(pl.multiple_of(j * PAT, PAT), PAT)
+        return work[rows, :PAT], work[rows, PAT:]
+
     def forward(j, _):
-        pr, pi = patch[j, 0], patch[j, 1]
+        pr, pi = window_of(j)
 
         def mode(m, _):
-            pr, pi = patch[j, 0], patch[j, 1]
+            pr, pi = window_of(j)
             qr, qi = probe[0, m], probe[1, m]
             er = qr * pr - qi * pi
             ei = qr * pi + qi * pr
@@ -248,7 +263,7 @@
             qr, qi = probe[0, m], probe[1, m]
             grad[j, 0] += qr * br + qi * bi
             grad[j, 1] += qr * bi - qi * br
-            pr, pi = patch[j, 0], patch[j, 1]
+            pr, pi = window_of(j)
             numer[0, m] += pr * br + pi * bi
             numer[1, m] += pr * bi - pi * br
             return 0
@@ -326,7 +341,8 @@
 
     def spread_plane(plane, j, block):
         rows = pl.ds(pl.multiple_of(j * PAT, PAT), PAT)
-        by = jnp.broadcast_to(shifts[pl.ds(NPAT + j, 1), :], (PAT, TILE))
+        by = jnp.broadcast_to(work[pl.ds(POWER + NPAT + j, 1), PAT:], (PAT, PAT)).astype(jnp.int32)
+        by = jnp.concatenate([by, by], axis=1)
         columns = jnp.where(along((PAT, TILE), 1) - along((PAT, TILE), 0) == by, 1.0, 0.0).astype(BF16)
         h, l = split(block)
         h, l = split(dot(h, columns) + dot(l, columns))
@@ -349,7 +365,7 @@
     def update(starts, count):
         chosen = []
         for j in range(NPAT):
-            by = jnp.broadcast_to(shifts[j:j + 1, :PAT], (count, PAT))
+            by = jnp.broadcast_to(work[POWER + j:POWER + j + 1, PAT:], (count, PAT)).astype(jnp.int32)
             away = along((count, PAT), 0) - along((count, PAT), 1)
             chosen.append(jnp.concatenate([jnp.where(away + start == by, 1.0, 0.0).astype(BF16) for start in starts], axis=0))
         chosen = jnp.concatenate(chosen, axis=1)
@@ -360,37 +376,56 @@
             for plane in range(2):
                 mid[plane, rows, :] = (obj[plane, rows, :] + sums[plane][here]) * inverse_weight
 
+    def dual(side, plane):
+        start = DUALS + (2 * side + plane) * EDGE
+        return work[start:start + EDGE, :]
+
     def mask_start():
+        wide = lambda ref, i: jnp.broadcast_to(ref[0:1, i:i + 1], (1, TILE))
+        number = along((1, TILE), 1) // BLOCK
+        first, second, count = wide(pieces, 0) == number, wide(pieces, 1) == number, wide(live, 0)
+        last = jnp.broadcast_to(me.region, (1, TILE)) >= 31
+        flag = lambda chosen: jnp.where(chosen, 1.0, 0.0).astype(F32)
+        active = flag(first & (count > 0)) + flag(second & (count > 1))
+        mask[0:1, :] = flag(first)
+        mask[1:2, :] = flag(second)
+        mask[2:3, :] = jnp.where(last, 0.0, active)
+        mask[3:8, :] = jnp.zeros((5, TILE), F32)
         send(mask, mask_in, edge_sems, 0, me.region_by(1))
 
     def edge_start():
         await_bytes(mask_in, edge_recv.at[0])
         for plane in range(2):
-            up[plane] = mid[plane, :EDGE] + dual_top[plane]
-            low[plane] = mid[plane, TILE - EDGE:] + dual_bottom[plane]
+            up[plane] = mid[plane, :EDGE] + dual(0, plane)
+            low[plane] = mid[plane, TILE - EDGE:] + dual(1, plane)
             up_sent[plane] = packed(up[plane], mask_in)
             low_sent[plane] = packed(low[plane], mask)
-        send(up_sent, from_below, edge_sems, 1, me.region_by(-1))
-        send(low_sent, from_above, edge_sems, 2, me.region_by(1))
+
+    def edge_send_plane(plane):
+        send(up_sent.at[plane], from_below.at[plane], edge_sems, 1 + plane, me.region_by(-1))
+        send(low_sent.at[plane], from_above.at[plane], edge_sems, 3 + plane, me.region_by(1))
 
     def edge_end():
-        await_bytes(from_below, edge_recv.at[1])
-        await_bytes(from_above, edge_recv.at[2])
         for plane in range(2):
+            await_bytes(from_below.at[plane], edge_recv.at[1 + plane])
+            await_bytes(from_above.at[plane], edge_recv.at[3 + plane])
             here = mid[plane, TILE - EDGE:]
             agreed = 0.5 * (low[plane] + unpacked(from_below[plane], mask))
             active = jnp.broadcast_to(mask[2:3, :], (EDGE, TILE)) > 0.5
-            bottom_out[plane] = jnp.where(active, dual_bottom[plane] + (here - agreed), dual_bottom[plane])
+            bottom_out[plane] = jnp.where(active, dual(1, plane) + (here - agreed), dual(1, plane))
             mid[plane, TILE - EDGE:] = jnp.where(active, agreed, here)
             here = mid[plane, :EDGE]
             agreed = 0.5 * (unpacked(from_above[plane], mask_in) + up[plane])
             active = jnp.broadcast_to(mask_in[2:3, :], (EDGE, TILE)) > 0.5
-            top_out[plane] = jnp.where(active, dual_top[plane] + (here - agreed), dual_top[plane])
+            top_out[plane] = jnp.where(active, dual(0, plane) + (here - agreed), dual(0, plane))
             mid[plane, :EDGE] = jnp.where(active, agreed, here)
 
-    loads[0].wait()
-    loads[1].wait()
+    wait_loads(0, 10)
+    wait_loads(15, 16)
     lax.fori_loop(0, 1, forward, 0)
+    wait_loads(10, 15)
+    wait_loads(16, 19)
+    denom[...] = work[POWER:POWER + PAT, :PAT]
     lax.fori_loop(1, 2, forward, 0)
     lax.fori_loop(2, 3, forward, 0)
     pl.semaphore_wait(barrier, 21)
@@ -414,36 +449,37 @@
     line_start(2)
     inverse(3, 2, 4)
     core_start(3)
-    denom_end()
     spread(0, 2)
     plane_start(1)
+    line_start(3)
     spread(2, 4)
-    line_start(3)
+    denom_end()
     back_start(0)
+    plane_start(2)
     spread_weights()
-    plane_start(2)
-    for load in loads[2:]:
-        load.wait()
+    wait_loads(19, LOADS)
     update((0, TILE - EDGE), EDGE)
+    plane_start(3)
     edge_start()
+    edge_send_plane(0)
+    update((EDGE,), TILE // 2 - EDGE)
     back_start(1)
-    update((EDGE,), TILE // 2 - EDGE)
-    plane_start(3)
+    back_line_start(0)
     update((TILE // 2,), TILE // 2 - EDGE)
-    back_line_start(0)
     back_start(2)
+    back_start(3)
+    edge_send_plane(1)
     back_line_start(1)
-    back_start(3)
     back_core_start(0)
     back_line_start(2)
+    back_line_start(3)
+    back_core_start(1)
     edge_end()
+    back_core_start(2)
     back_end(0)
-    back_core_start(1)
-    back_line_start(3)
+    back_core_start(3)
     back_end(1)
-    back_core_start(2)
     back_end(2)
-    back_core_start(3)
     back_end(3)
 
     for m in range(SUMS):
@@ -455,15 +491,33 @@
         await_bytes(fresh.at[0, m, pl.ds(0, 192), :], back_line_send.at[m])
         await_bytes(fresh.at[0, m], back_core_send.at[m])
     await_bytes(mask_in, edge_send.at[0])
-    await_bytes(up_sent, edge_send.at[1])
-    await_bytes(low_sent, edge_send.at[2])
+    for plane in range(2):
+        await_bytes(up_sent.at[plane], edge_send.at[1 + plane])
+        await_bytes(low_sent.at[plane], edge_send.at[3 + plane])
+
+
+def write_out(mid, probe, top, bottom, mid_out, probe_out, top_out, bottom_out, sems):
+    copies = []
+    for plane in range(2):
+        copies.append((top.at[plane], top_out.at[plane]))
+        copies.append((bottom.at[plane], bottom_out.at[plane]))
+        for i in range(2):
+            rows = pl.ds(i * PAT, PAT)
+            copies.append((mid.at[plane, rows], mid_out.at[plane, rows]))
+            copies.append((probe.at[plane, pl.ds(2 * i, 2)], probe_out.at[plane, pl.ds(2 * i, 2)]))
+    copies = [pltpu.make_async_copy(source, target, sems.at[i]) for i, (source, target) in enumerate(copies)]
+    for copy in copies:
+        copy.start()
+    for copy in copies:
+        copy.wait()
 
 
 def local(object_field, probe, amplitudes, positions, dual_top, dual_bottom, pieces, live):
-    tab, perm = tables()
+    tab = tables()
     vmem = pl.BlockSpec(memory_space=pltpu.VMEM)
     smem = pl.BlockSpec(memory_space=pltpu.SMEM)
-    far = pl.BlockSpec(memory_space=pl.ANY)
+    far = pl.BlockSpec(memory_space=pltpu.HBM)
+    anywhere = pl.BlockSpec(memory_space=pl.ANY)
     buf = lambda *shape: pltpu.VMEM(shape, F32)
     half = lambda *shape: pltpu.VMEM(shape, BF16)
     dma = lambda *shape: pltpu.SemaphoreType.DMA(shape)
@@ -471,27 +525,34 @@
     shape = lambda *dims: jax.ShapeDtypeStruct(dims, F32)
     prepared = pl.pallas_call(
         prepare,
-        out_shape=(shape(NPAT, 2, PAT, PAT), jax.ShapeDtypeStruct((2 * NPAT, TILE), jnp.int32), shape(8, TILE), shape(PAT, PAT)),
-        in_specs=[smem] * 3 + [far],
-        out_specs=(vmem,) * 4,
-        scratch_shapes=[buf(2, TILE, TILE), dma(4)],
-        compiler_params=pltpu.CompilerParams(vmem_limit_bytes=16 * 1024 * 1024),
-    )(positions.T, pieces.T, live, object_field)
-    return pl.pallas_call(
+        out_shape=shape(DUALS + PAT, TILE),
+        in_specs=[smem] + [far] * 3,
+        out_specs=far,
+        scratch_shapes=[buf(DUALS + PAT, TILE), buf(2, TILE, TILE), dma(13)],
+        compiler_params=pltpu.CompilerParams(vmem_limit_bytes=60 * 1024 * 1024),
+    )(positions.T, object_field, dual_top, dual_bottom)
+    results = pl.pallas_call(
         kernel,
         out_shape=(shape(2, TILE, TILE), shape(2, MODES, PAT, PAT), shape(*edge), shape(*edge)),
-        in_specs=[vmem] * 6 + [far] * 5,
+        in_specs=[far] * 3 + [vmem] * 2 + [far] * 2,
         out_specs=(vmem,) * 4,
         scratch_shapes=[
             buf(MODES * NPAT, 2, PAT, PAT), buf(NPAT, 2, PAT, PAT), buf(NPAT, 2, PAT, PAT),
             half(3, NPAT * PAT, TILE), half(3, NPAT * PAT, TILE), buf(2, MODES, PAT, PAT),
             buf(SUMS, PAT, PAT), buf(SUMS, PAT, PAT), buf(SUMS, 3, 64, PAT), buf(SUMS, 16, 8, HALF), buf(SUMS, 15, 8, HALF),
             buf(MODES, 16, 8, HALF), buf(2, MODES, PAT, PAT), buf(8, HALF),
-            buf(2, TILE, TILE), buf(NPAT, PAT, PAT), half(2, PAT, PAT), buf(*edge), buf(*edge),
-            buf(8, TILE), buf(*edge), buf(*edge), buf(*sent), buf(*sent), buf(*sent), buf(*sent),
-        ] + [dma(SUMS)] * 6 + [dma(MODES)] * 6 + [dma(3), dma(3), dma(5)],
+            buf(DUALS + PAT, TILE), buf(PAT, PAT), buf(2, MODES, PAT, PAT), half(2, 2, 2, PAT, PAT), buf(2, TILE, TILE), buf(NPAT, PAT, PAT), half(2, PAT, PAT), buf(8, TILE), buf(8, TILE), buf(*edge), buf(*edge), buf(*sent), buf(*sent), buf(*sent), buf(*sent),
+        ] + [dma(SUMS)] * 6 + [dma(MODES)] * 6 + [dma(5), dma(5), dma(LOADS)],
         compiler_params=pltpu.CompilerParams(vmem_limit_bytes=LIMIT * 1024 * 1024, collective_id=0, has_side_effects=True),
-    )(*prepared, probe, jnp.asarray(tab), object_field, amplitudes, jnp.asarray(perm), dual_top, dual_bottom)
+    )(prepared, probe, jnp.asarray(tab), pieces.T, live, object_field, amplitudes)
+    return pl.pallas_call(
+        write_out,
+        out_shape=(shape(2, TILE, TILE), shape(2, MODES, PAT, PAT), shape(*edge), shape(*edge)),
+        in_specs=[anywhere] * 4,
+        out_specs=(far,) * 4,
+        scratch_shapes=[dma(12)],
+        compiler_params=pltpu.CompilerParams(vmem_limit_bytes=1024 * 1024),
+    )(*results)
 
 
 def solution(mesh):

time: 71.3 us -> 64.9 us (0.910)
  local copies, waits for them, and re-layouts: 9.82 us -> 0.02 us
  Pallas kernels: 59.9 us -> 63.3 us
    unnamed x20 -> x6, local copies, waits for them, and re-layouts: 9.82 us -> 0.02 us
    pallas_call x1 -> x2, Pallas kernels: 1.65 us -> 6.77 us  [the longest x1 4.49 us: local(): pl.pallas_call(prepare, out_shape=shape(DUALS + PAT, TILE), in_specs=[sme...]
    pallas_call x1, Pallas kernels: 58.2 us -> 56.5 us  [local(): pl.pallas_call(kernel, out_shape=(shape(2, TILE, TILE), shape(2, MODES, P...]
where the time goes in v2:
time: 64.9 us; the launch traced here: 64.8 us
  Pallas kernels  63.3 us (98%)
  between operations  1.5 us (2%)
    pallas_call x1, Pallas kernels, local(): pl.pallas_call(kernel, out_shape=(shape(2, TILE, TILE), shape(2, MODES, P...  56.5 us
    pallas_call x1, Pallas kernels, local(): pl.pallas_call(prepare, out_shape=shape(DUALS + PAT, TILE), in_specs=[sme...  4.49 us
    pallas_call x1, Pallas kernels, local(): pl.pallas_call(write_out, out_shape=(shape(2, TILE, TILE), shape(2, MODES...  2.28 us

profile of v2, /device:TPU:1, one launch (start us, length us, event | category | flops | bytes accessed | tf_op | source)
XLA Modules:
  0.0 64.8 jit_solution(1970447552688604961)
XLA Ops:
  1.3 0.0 copy-start
  1.3 0.0 copy-start.1
  1.3 0.0 copy-start.2
  1.3 4.5 %shard_map.120.far_work = f32[1536,512]{1,0:T(8,128)} custom-call(s32[2,4]{1,0:T(2,128)} %bitcast.3, f32[2,512,512]{2,1,0:T(8,128)} %far_obj.3, f32[2,64,512]{2,1,0:T(8,128)} %far_top.1, f32[2,64,512]{2,1,0:T(8,128)} %far_bottom.1), custom_call_target="tpu_custom_call" | custom-call | tf_op jit(solution)/shard_map/pallas_call | solution.py:526
  5.8 0.0 copy-done
  5.8 0.0 copy-done.1
  5.8 0.0 copy-done.2
  5.8 56.5 %shard_map.121 = (f32[2,512,512]{2,1,0:T(8,128)S(1)}, f32[2,4,256,256]{3,2,1,0:T(8,128)S(1)}, f32[2,64,512]{2,1,0:T(8,128)S(1)}, f32[2,64,512]{2,1,0:T(8,128)S(1)}) custom-call(f32[1536,512]{1,0:T(8,128)} %shard_map.120.far_work, f32[2,4,256,256]{3,2,1,0:T(8,128)} %far_probe.1, bf16[2,2,2,256,256]{4,3,2,1,0:T(8,128)(2,1)S(1)} %copy-done.1, ...), custom_call_target="tpu_custom_call" | custom-call | tf_op jit(solution)/shard_map/pallas_call | solution.py:534
  62.3 2.3 %shard_map.122 = (f32[2,512,512]{2,1,0:T(8,128)}, f32[2,4,256,256]{3,2,1,0:T(8,128)}, f32[2,64,512]{2,1,0:T(8,128)}, f32[2,64,512]{2,1,0:T(8,128)}) custom-call(f32[2,512,512]{2,1,0:T(8,128)S(1)} %get-tuple-element.8.mid, f32[2,4,256,256]{3,2,1,0:T(8,128)S(1)} %get-tuple-element.9.probe, f32[2,64,512]{2,1,0:T(8,128)S(1)} %get-tuple-element.10.top, ...), custom_call_target="tpu_custom_call" | custom-call | tf_op jit(solution)/shard_map/pallas_call | solution.py:548
Async XLA Ops:
  1.3 4.5 %copy-start = (f32[4,256,256]{2,1,0:T(8,128)S(1)}, f32[4,256,256]{2,1,0:T(8,128)}, u32[]{:S(2)}) copy-start(f32[4,256,256]{2,1,0:T(8,128)} %far_amp.1) | copy-start | bytes 3145732
  1.3 4.5 %copy-start.1 = (bf16[2,2,2,256,256]{4,3,2,1,0:T(8,128)(2,1)S(1)}, bf16[2,2,2,256,256]{4,3,2,1,0:T(8,128)(2,1)}, u32[]{:S(2)}) copy-start(bf16[2,2,2,256,256]{4,3,2,1,0:T(8,128)(2,1)} %constant.2.clone.far_tab) | copy-start | bytes 3145732
  1.3 4.5 %copy-start.2 = (s32[2,1]{0,1:T(1,128)S(1)}, s32[2,1]{0,1:T(1,128)}, u32[]{:S(2)}) copy-start(s32[2,1]{0,1:T(1,128)} %param.15) | copy-start | bytes 28

commit v3 on v2

--- a/solution.py
+++ b/solution.py
@@ -41,13 +41,13 @@
     return h, (a - h.astype(F32)).astype(BF16)
 
 
-def right(a, t, d, p):
-    h, l = split(a)
+def right_of(parts, t, d, p):
+    h, l = parts
     return dot(h, t[d, p, 1]) + dot(h, t[d, p, 0]) + dot(l, t[d, p, 0])
 
 
-def left(t, d, p, a):
-    h, l = split(a)
+def left_of(t, d, p, parts):
+    h, l = parts
     return dot(t[d, p, 0], l) + dot(t[d, p, 1], h) + dot(t[d, p, 0], h)
 
 
@@ -172,7 +172,7 @@
 def kernel(
     far_work, far_probe, far_tab, pieces, live, far_obj, far_amp,
     mid, probe_out, top_out, bottom_out,
-    far, factor, grad, spread_hi, spread_lo, numer,
+    far, factor, spread_hi, spread_lo, numer,
     from_core, part, from_line, block, from_plane, tiles, fresh, scale,
     work, denom, probe, tab, obj, amp, perm, mask, mask_in, up, low, up_sent, low_sent, from_below, from_above,
     core_send, core_recv, line_send, line_recv, plane_send, plane_recv,
@@ -208,33 +208,37 @@
         place = along((PAT, PAT), axis)
         source = 2 * (place & (HALF - 1)) + (place >> 7)
         perm[i] = jnp.where(along((PAT, PAT), other) == source, 1.0, 0.0).astype(BF16)
-    grad[...] = jnp.zeros_like(grad)
-
     def window_of(j):
         rows = pl.ds(pl.multiple_of(j * PAT, PAT), PAT)
         return work[rows, :PAT], work[rows, PAT:]
 
-    def forward(j, _):
-        pr, pi = window_of(j)
-
-        def mode(m, _):
+    def forward(j):
+        def exit_of(m):
             pr, pi = window_of(j)
             qr, qi = probe[0, m], probe[1, m]
             er = qr * pr - qi * pi
             ei = qr * pi + qi * pr
             lo = jnp.concatenate([er[:, :HALF], ei[:, :HALF]], axis=1)
             hi = jnp.concatenate([er[:, HALF:], ei[:, HALF:]], axis=1)
-            y0 = right(lo + hi, tab, 0, 0)
-            y1 = right(lo - hi, tab, 0, 1)
+            return split(lo + hi), split(lo - hi)
+
+        def first_of(parts):
+            y0 = right_of(parts[0], tab, 0, 0)
+            y1 = right_of(parts[1], tab, 0, 1)
             yr = jnp.concatenate([y0[:, :HALF], y1[:, :HALF]], axis=1)
             yi = jnp.concatenate([y0[:, HALF:], y1[:, HALF:]], axis=1)
             top = jnp.concatenate([yr[:HALF], yi[:HALF]], axis=0)
             bot = jnp.concatenate([yr[HALF:], yi[HALF:]], axis=0)
-            far[m * NPAT + j, 0] = left(tab, 1, 0, top + bot)
-            far[m * NPAT + j, 1] = left(tab, 1, 1, top - bot)
-            return 0
-
-        lax.fori_loop(0, MODES, mode, 0, unroll=True)
+            return split(top + bot), split(top - bot)
+
+        def second_of(m, parts):
+            far[m * NPAT + j, 0] = left_of(tab, 1, 0, parts[0])
+            far[m * NPAT + j, 1] = left_of(tab, 1, 1, parts[1])
+
+        exits = [exit_of(m) for m in range(MODES)]
+        halfway = [first_of(parts) for parts in exits]
+        for m in range(MODES):
+            second_of(m, halfway[m])
         h, l = split(amp[j])
         h, l = split(dot(h, perm[0]) + dot(l, perm[0]))
         full = dot(perm[1], h) + dot(perm[1], l)
@@ -246,32 +250,40 @@
             f = full[q * HALF:(q + 1) * HALF] / jnp.maximum(jnp.sqrt(power), 0.5)
             factor[j, q, :HALF] = f
             factor[j, q, HALF:] = f
-        return 0
 
     def inverse(m, first, last):
-        def one(j, _):
-            g0 = left(tab, 0, 0, far[m * NPAT + j, 0] * factor[j, 0])
-            g1 = left(tab, 0, 1, far[m * NPAT + j, 1] * factor[j, 1])
+        positions = range(first, last)
+
+        def fixed_of(j):
+            return split(far[m * NPAT + j, 0] * factor[j, 0]), split(far[m * NPAT + j, 1] * factor[j, 1])
+
+        def first_of(parts):
+            g0 = left_of(tab, 0, 0, parts[0])
+            g1 = left_of(tab, 0, 1, parts[1])
             top, bot = g0 + g1, g0 - g1
             xr = jnp.concatenate([top[:HALF], bot[:HALF]], axis=0)
             xi = jnp.concatenate([top[HALF:], bot[HALF:]], axis=0)
-            b0 = right(jnp.concatenate([xr[:, :HALF], xi[:, :HALF]], axis=1), tab, 1, 0)
-            b1 = right(jnp.concatenate([xr[:, HALF:], xi[:, HALF:]], axis=1), tab, 1, 1)
+            a0 = jnp.concatenate([xr[:, :HALF], xi[:, :HALF]], axis=1)
+            a1 = jnp.concatenate([xr[:, HALF:], xi[:, HALF:]], axis=1)
+            return split(a0), split(a1)
+
+        def back_of(j, parts):
+            b0 = right_of(parts[0], tab, 1, 0)
+            b1 = right_of(parts[1], tab, 1, 1)
             lo, hi = b0 + b1, b0 - b1
             br = jnp.concatenate([lo[:, :HALF], hi[:, :HALF]], axis=1)
             bi = jnp.concatenate([lo[:, HALF:], hi[:, HALF:]], axis=1)
-            qr, qi = probe[0, m], probe[1, m]
-            grad[j, 0] += qr * br + qi * bi
-            grad[j, 1] += qr * bi - qi * br
+            far[m * NPAT + j, 0] = br
+            far[m * NPAT + j, 1] = bi
             pr, pi = window_of(j)
-            numer[0, m] += pr * br + pi * bi
-            numer[1, m] += pr * bi - pi * br
-            return 0
-
-        if first == 0:
-            numer[0, m] = jnp.zeros((PAT, PAT), F32)
-            numer[1, m] = jnp.zeros((PAT, PAT), F32)
-        lax.fori_loop(first, last, one, 0, unroll=True)
+            real, imag = pr * br + pi * bi, pr * bi - pi * br
+            numer[0, m] = real if j == 0 else numer[0, m] + real
+            numer[1, m] = imag if j == 0 else numer[1, m] + imag
+
+        fixed = [fixed_of(j) for j in positions]
+        halfway = [first_of(parts) for parts in fixed]
+        for j, parts in zip(positions, halfway):
+            back_of(j, parts)
 
     line_rows = pl.ds(pl.multiple_of(me.v * 64, 64), 64)
     core_sems, line_sems, plane_sems = (core_send, core_recv), (line_send, line_recv), (plane_send, plane_recv)
@@ -351,8 +363,13 @@
 
     def spread(first, last):
         def one(j, _):
-            spread_plane(0, j, grad[j, 0])
-            spread_plane(1, j, grad[j, 1])
+            real, imag = jnp.zeros((PAT, PAT), F32), jnp.zeros((PAT, PAT), F32)
+            for m in range(MODES):
+                br, bi, qr, qi = far[m * NPAT + j, 0], far[m * NPAT + j, 1], probe[0, m], probe[1, m]
+                real = real + qr * br + qi * bi
+                imag = imag + qr * bi - qi * br
+            spread_plane(0, j, real)
+            spread_plane(1, j, imag)
             return 0
 
         lax.fori_loop(first, last, one, 0, unroll=True)
@@ -422,64 +439,65 @@
 
     wait_loads(0, 10)
     wait_loads(15, 16)
-    lax.fori_loop(0, 1, forward, 0)
+    forward(0)
     wait_loads(10, 15)
     wait_loads(16, 19)
     denom[...] = work[POWER:POWER + PAT, :PAT]
-    lax.fori_loop(1, 2, forward, 0)
-    lax.fori_loop(2, 3, forward, 0)
+    forward(1)
+    forward(2)
     pl.semaphore_wait(barrier, 21)
     mask_start()
     core_start(MODES)
-    lax.fori_loop(3, 4, forward, 0)
+    forward(3)
     line_start(MODES)
     inverse(0, 0, 4)
     core_start(0)
     inverse(1, 0, 2)
     line_start(0)
-    plane_start(MODES)
     inverse(1, 2, 4)
     core_start(1)
+    plane_start(MODES)
     inverse(2, 0, 2)
     line_start(1)
     inverse(2, 2, 4)
     core_start(2)
+    inverse(3, 0, 2)
     plane_start(0)
-    inverse(3, 0, 2)
     line_start(2)
     inverse(3, 2, 4)
     core_start(3)
-    spread(0, 2)
+    spread(0, 1)
+    line_start(3)
     plane_start(1)
-    line_start(3)
+    denom_end()
+    spread(1, 2)
     spread(2, 4)
-    denom_end()
     back_start(0)
     plane_start(2)
     spread_weights()
     wait_loads(19, LOADS)
     update((0, TILE - EDGE), EDGE)
+    edge_start()
     plane_start(3)
-    edge_start()
+    back_start(1)
+    update((EDGE,), TILE // 2 - EDGE)
+    back_line_start(0)
+    back_start(2)
+    update((TILE // 2,), TILE // 2 - EDGE)
+    back_start(3)
     edge_send_plane(0)
-    update((EDGE,), TILE // 2 - EDGE)
-    back_start(1)
-    back_line_start(0)
-    update((TILE // 2,), TILE // 2 - EDGE)
-    back_start(2)
-    back_start(3)
-    edge_send_plane(1)
     back_line_start(1)
     back_core_start(0)
     back_line_start(2)
     back_line_start(3)
+    edge_send_plane(1)
     back_core_start(1)
-    edge_end()
     back_core_start(2)
     back_end(0)
     back_core_start(3)
     back_end(1)
     back_end(2)
+    edge_end()
     back_end(3)
 
     for m in range(SUMS):
@@ -537,7 +555,7 @@
         in_specs=[far] * 3 + [vmem] * 2 + [far] * 2,
         out_specs=(vmem,) * 4,
         scratch_shapes=[
-            buf(MODES * NPAT, 2, PAT, PAT), buf(NPAT, 2, PAT, PAT), buf(NPAT, 2, PAT, PAT),
+            buf(MODES * NPAT, 2, PAT, PAT), buf(NPAT, 2, PAT, PAT),
             half(3, NPAT * PAT, TILE), half(3, NPAT * PAT, TILE), buf(2, MODES, PAT, PAT),
             buf(SUMS, PAT, PAT), buf(SUMS, PAT, PAT), buf(SUMS, 3, 64, PAT), buf(SUMS, 16, 8, HALF), buf(SUMS, 15, 8, HALF),
             buf(MODES, 16, 8, HALF), buf(2, MODES, PAT, PAT), buf(8, HALF),

time: 64.9 us -> 59 us (0.909)
  Pallas kernels: 63.3 us -> 56.9 us
    pallas_call x1, Pallas kernels: 56.5 us -> 50.1 us  [local(): pl.pallas_call(kernel, out_shape=(shape(2, TILE, TILE), shape(2, MODES, P...]
where the time goes in v3:
time: 59 us; the launch traced here: 58.4 us
  Pallas kernels  56.9 us (96%)
  between operations  1.5 us (3%)
    pallas_call x1, Pallas kernels, local(): pl.pallas_call(kernel, out_shape=(shape(2, TILE, TILE), shape(2, MODES, P...  50.1 us
    pallas_call x1, Pallas kernels, local(): pl.pallas_call(prepare, out_shape=shape(DUALS + PAT, TILE), in_specs=[sme...  4.49 us
    pallas_call x1, Pallas kernels, local(): pl.pallas_call(write_out, out_shape=(shape(2, TILE, TILE), shape(2, MODES...  2.28 us

profile of v3, /device:TPU:1, one launch (start us, length us, event | category | flops | bytes accessed | tf_op | source)
XLA Modules:
  0.0 58.4 jit_solution(8205328863539967389)
XLA Ops:
  1.3 0.0 copy-start
  1.3 0.0 copy-start.1
  1.3 0.0 copy-start.2
  1.3 4.5 %shard_map.120.far_work = f32[1536,512]{1,0:T(8,128)} custom-call(s32[2,4]{1,0:T(2,128)} %bitcast.3, f32[2,512,512]{2,1,0:T(8,128)} %far_obj.3, f32[2,64,512]{2,1,0:T(8,128)} %far_top.1, f32[2,64,512]{2,1,0:T(8,128)} %far_bottom.1), custom_call_target="tpu_custom_call" | custom-call | tf_op jit(solution)/shard_map/pallas_call | solution.py:544
  5.8 0.0 copy-done
  5.8 0.0 copy-done.1
  5.8 0.0 copy-done.2
  5.8 50.1 %shard_map.121 = (f32[2,512,512]{2,1,0:T(8,128)S(1)}, f32[2,4,256,256]{3,2,1,0:T(8,128)S(1)}, f32[2,64,512]{2,1,0:T(8,128)S(1)}, f32[2,64,512]{2,1,0:T(8,128)S(1)}) custom-call(f32[1536,512]{1,0:T(8,128)} %shard_map.120.far_work, f32[2,4,256,256]{3,2,1,0:T(8,128)} %far_probe.1, bf16[2,2,2,256,256]{4,3,2,1,0:T(8,128)(2,1)S(1)} %copy-done.1, ...), custom_call_target="tpu_custom_call" | custom-call | tf_op jit(solution)/shard_map/pallas_call | solution.py:552
  56.0 2.3 %shard_map.122 = (f32[2,512,512]{2,1,0:T(8,128)}, f32[2,4,256,256]{3,2,1,0:T(8,128)}, f32[2,64,512]{2,1,0:T(8,128)}, f32[2,64,512]{2,1,0:T(8,128)}) custom-call(f32[2,512,512]{2,1,0:T(8,128)S(1)} %get-tuple-element.8.mid, f32[2,4,256,256]{3,2,1,0:T(8,128)S(1)} %get-tuple-element.9.probe, f32[2,64,512]{2,1,0:T(8,128)S(1)} %get-tuple-element.10.top, ...), custom_call_target="tpu_custom_call" | custom-call | tf_op jit(solution)/shard_map/pallas_call | solution.py:566
Async XLA Ops:
  1.3 4.5 %copy-start = (f32[4,256,256]{2,1,0:T(8,128)S(1)}, f32[4,256,256]{2,1,0:T(8,128)}, u32[]{:S(2)}) copy-start(f32[4,256,256]{2,1,0:T(8,128)} %far_amp.1) | copy-start | bytes 3145732
  1.3 4.5 %copy-start.1 = (bf16[2,2,2,256,256]{4,3,2,1,0:T(8,128)(2,1)S(1)}, bf16[2,2,2,256,256]{4,3,2,1,0:T(8,128)(2,1)}, u32[]{:S(2)}) copy-start(bf16[2,2,2,256,256]{4,3,2,1,0:T(8,128)(2,1)} %constant.2.clone.far_tab) | copy-start | bytes 3145732
  1.3 4.5 %copy-start.2 = (s32[2,1]{0,1:T(1,128)S(1)}, s32[2,1]{0,1:T(1,128)}, u32[]{:S(2)}) copy-start(s32[2,1]{0,1:T(1,128)} %param.15) | copy-start | bytes 28

commit v4 on v3

--- a/solution.py
+++ b/solution.py
@@ -89,8 +89,11 @@
     for j in range(NPAT):
         work[POWER + j:POWER + j + 1, PAT:] = jnp.full((1, PAT), pos[0, j].astype(F32), F32)
         work[POWER + NPAT + j:POWER + NPAT + j + 1, PAT:] = jnp.full((1, PAT), pos[1, j].astype(F32), F32)
-    for copy in loads[:4]:
+    for copy in loads:
         copy.wait()
+    rows = pl.ds(DUALS, PAT)
+    stores.append(pltpu.make_async_copy(work.at[rows], work_out.at[rows], sems.at[13]))
+    stores[-1].start()
     total = jnp.zeros((PAT, PAT), F32)
     for j in range(NPAT):
         pr, pi = window(obj, 0, pos[0, j], pos[1, j]), window(obj, 1, pos[0, j], pos[1, j])
@@ -101,9 +104,7 @@
         stores[-1].start()
         total = total + pr * pr + pi * pi
     work[POWER:POWER + PAT, :PAT] = total
-    for copy in loads[4:]:
-        copy.wait()
-    rows = pl.ds(POWER, 2 * PAT)
+    rows = pl.ds(POWER, PAT)
     stores.append(pltpu.make_async_copy(work.at[rows], work_out.at[rows], sems.at[12]))
     stores[-1].start()
     for copy in stores:
@@ -480,17 +481,17 @@
     edge_start()
     plane_start(3)
     back_start(1)
+    back_line_start(0)
     update((EDGE,), TILE // 2 - EDGE)
-    back_line_start(0)
     back_start(2)
+    back_start(3)
     update((TILE // 2,), TILE // 2 - EDGE)
-    back_start(3)
+    back_line_start(1)
     edge_send_plane(0)
-    back_line_start(1)
+    back_line_start(2)
+    edge_send_plane(1)
     back_core_start(0)
-    back_line_start(2)
     back_line_start(3)
-    edge_send_plane(1)
     back_core_start(1)
     back_core_start(2)
     back_end(0)
@@ -546,7 +547,7 @@
         out_shape=shape(DUALS + PAT, TILE),
         in_specs=[smem] + [far] * 3,
         out_specs=far,
-        scratch_shapes=[buf(DUALS + PAT, TILE), buf(2, TILE, TILE), dma(13)],
+        scratch_shapes=[buf(DUALS + PAT, TILE), buf(2, TILE, TILE), dma(14)],
         compiler_params=pltpu.CompilerParams(vmem_limit_bytes=60 * 1024 * 1024),
     )(positions.T, object_field, dual_top, dual_bottom)
     results = pl.pallas_call(

time: 59 us -> 58.7 us (level)
  no operation moved by 1% of the time
where the time goes in v4:
time: 58.7 us; the launch traced here: 58.6 us
  Pallas kernels  57.1 us (97%)
  between operations  1.5 us (3%)
    pallas_call x1, Pallas kernels, local(): pl.pallas_call(kernel, out_shape=(shape(2, TILE, TILE), shape(2, MODES, P...  50.3 us
    pallas_call x1, Pallas kernels, local(): pl.pallas_call(prepare, out_shape=shape(DUALS + PAT, TILE), in_specs=[sme...  4.46 us
    pallas_call x1, Pallas kernels, local(): pl.pallas_call(write_out, out_shape=(shape(2, TILE, TILE), shape(2, MODES...  2.28 us

profile of v4, /device:TPU:1, one launch (start us, length us, event | category | flops | bytes accessed | tf_op | source)
XLA Modules:
  0.0 58.6 jit_solution(17910592669132084894)
XLA Ops:
  1.3 0.0 copy-start
  1.3 0.0 copy-start.1
  1.3 0.0 copy-start.2
  1.3 4.5 %shard_map.120.far_work = f32[1536,512]{1,0:T(8,128)} custom-call(s32[2,4]{1,0:T(2,128)} %bitcast.3, f32[2,512,512]{2,1,0:T(8,128)} %far_obj.3, f32[2,64,512]{2,1,0:T(8,128)} %far_top.1, f32[2,64,512]{2,1,0:T(8,128)} %far_bottom.1), custom_call_target="tpu_custom_call" | custom-call | tf_op jit(solution)/shard_map/pallas_call | solution.py:545
  5.8 0.0 copy-done
  5.8 0.0 copy-done.1
  5.8 0.0 copy-done.2
  5.8 50.3 %shard_map.121 = (f32[2,512,512]{2,1,0:T(8,128)S(1)}, f32[2,4,256,256]{3,2,1,0:T(8,128)S(1)}, f32[2,64,512]{2,1,0:T(8,128)S(1)}, f32[2,64,512]{2,1,0:T(8,128)S(1)}) custom-call(f32[1536,512]{1,0:T(8,128)} %shard_map.120.far_work, f32[2,4,256,256]{3,2,1,0:T(8,128)} %far_probe.1, bf16[2,2,2,256,256]{4,3,2,1,0:T(8,128)(2,1)S(1)} %copy-done.1, ...), custom_call_target="tpu_custom_call" | custom-call | tf_op jit(solution)/shard_map/pallas_call | solution.py:553
  56.1 2.3 %shard_map.122 = (f32[2,512,512]{2,1,0:T(8,128)}, f32[2,4,256,256]{3,2,1,0:T(8,128)}, f32[2,64,512]{2,1,0:T(8,128)}, f32[2,64,512]{2,1,0:T(8,128)}) custom-call(f32[2,512,512]{2,1,0:T(8,128)S(1)} %get-tuple-element.8.mid, f32[2,4,256,256]{3,2,1,0:T(8,128)S(1)} %get-tuple-element.9.probe, f32[2,64,512]{2,1,0:T(8,128)S(1)} %get-tuple-element.10.top, ...), custom_call_target="tpu_custom_call" | custom-call | tf_op jit(solution)/shard_map/pallas_call | solution.py:567
Async XLA Ops:
  1.3 4.5 %copy-start = (f32[4,256,256]{2,1,0:T(8,128)S(1)}, f32[4,256,256]{2,1,0:T(8,128)}, u32[]{:S(2)}) copy-start(f32[4,256,256]{2,1,0:T(8,128)} %far_amp.1) | copy-start | bytes 3145732
  1.3 4.5 %copy-start.1 = (bf16[2,2,2,256,256]{4,3,2,1,0:T(8,128)(2,1)S(1)}, bf16[2,2,2,256,256]{4,3,2,1,0:T(8,128)(2,1)}, u32[]{:S(2)}) copy-start(bf16[2,2,2,256,256]{4,3,2,1,0:T(8,128)(2,1)} %constant.2.clone.far_tab) | copy-start | bytes 3145732
  1.3 4.5 %copy-start.2 = (s32[2,1]{0,1:T(1,128)S(1)}, s32[2,1]{0,1:T(1,128)}, u32[]{:S(2)}) copy-start(s32[2,1]{0,1:T(1,128)} %param.15) | copy-start | bytes 28
